TPU v7x, 256 devices: a whole 4x4x8 slice. The times are simulated.
256 devices in a mesh: row: 8 (over x, core), col: 32 (over y, z).
Axes of the slice: x: 4, y: 4, z: 8, core: 2. Of those that a mesh axis runs over, the one named last changes fastest.
Arguments:
- a_block: float32 [4, 4096, 16384], P(None, 'row', 'col'), may hold values from -6 to 6
- l_panel: float32 [1024, 4, 4096], P('col', None, 'row'), may hold values from -0.1875 to 0.1875
- inverses: float32 [2, 512, 512], replicated, as said below
Outputs:
- reduced: float32 [4, 4096, 16384], P(None, 'row', 'col')
- right_out: float32 [1024, 4, 4096], P('col', None, 'row')
Inputs may be any that keep to these rules, and one draw needn't show every extreme that they name: Each inverses[t] is lower triangular with diagonal entries from 1 to 2.5.
All inputs are finite; a program needn't handle non-finite values.
Results may differ from a plain program's by a relative error of at most 0.000071.
Values sent between devices are 32-bit elements; how exact they have to be, the bound alone decides.
No kernel may reach another device: no remote copies, remote signals or barrier semaphores. Data moves between devices by JAX's collectives and lax.ppermute only.
A program may use at most 128 MiB of HBM per device.

v0:
```python
import jax
import jax.numpy as jnp
from jax import lax
from jax.sharding import PartitionSpec as P


def broadcast(block, axis, owner):
    block = jnp.where(lax.axis_index(axis) == owner, block, jnp.zeros_like(block))
    return lax.psum(block, axis)


def product(left, right_side):
    return jnp.dot(
        left, right_side, precision=lax.Precision.HIGHEST, preferred_element_type=jnp.float32
    )


def on_device(a_block, l_panel, inverses):
    highest = lax.Precision.HIGHEST
    cycles, tile_rows, local_cols = a_block.shape
    grid_row = lax.axis_index("row")
    row_count = lax.axis_size("row")
    leading = a_block[0]
    l_columns = lax.all_gather(l_panel, "col", axis=0, tiled=True)
    lead_cols = l_columns[:, 0, :]
    first_candidate = product(inverses[0], leading)
    w_first = broadcast(first_candidate, "row", 0)
    coupling = jnp.einsum("kr,kj->rj", lead_cols[:tile_rows], w_first, precision=highest)
    second_candidate = product(inverses[1], leading - coupling)
    w_second = broadcast(second_candidate, "row", 1)
    panels = jnp.concatenate([w_first, w_second], axis=0)
    remaining = a_block - jnp.einsum("kcr,kj->crj", l_columns, panels, precision=highest)
    l_leading = l_columns[:tile_rows]
    top_tile = jnp.where(grid_row == 0, w_first, jnp.where(grid_row == 1, w_second, remaining[0]))
    reduced = remaining.at[0].set(top_tile)
    exchanged = lax.all_to_all(panels, "col", split_axis=0, concat_axis=1, tiled=True)
    own_count = exchanged.shape[0]
    grouped = exchanged.reshape(own_count, cycles, row_count, tile_rows)
    own_rows = lax.dynamic_index_in_dim(grouped, grid_row, 2, keepdims=False)
    y_candidate = product(own_rows[:, 0, :], inverses[0].T)
    y_first = broadcast(y_candidate, "row", 0)
    right_out = own_rows - jnp.einsum("kn,ncr->kcr", y_first, l_leading, precision=highest)
    first_block = jnp.where(grid_row == 0, y_first, right_out[:, 0, :])
    right_out = right_out.at[:, 0, :].set(first_block)
    return (reduced, right_out)


def solution(mesh):
    return jax.shard_map(
        on_device,
        mesh=mesh,
        in_specs=(P(None, "row", "col"), P("col", None, "row"), P()),
        out_specs=(P(None, "row", "col"), P("col", None, "row")),
        check_vma=False,
    )
```

profile of v0, /device:TPU:1, one launch (start us, length us, event | category | flops | bytes accessed | tf_op | source)
XLA Modules:
  0.0 326.2 jit_solution(12060875012828012840)
XLA Ops:
  8.0 0.0 copy-start.3
  8.0 0.0 all-reduce.4.cloned.1.call-start
  8.1 0.0 copy-start.1
  8.1 4.5 %convolution_select_fusion.1 = f32[512,512]{1,0:T(8,128)} fusion(f32[4,512,512]{2,1,0:T(8,128)} %param.7, f32[2,512,512]{2,1,0:T(8,128)} %param.9, pred[]{:T(512)S(6)} %eq.4), kind=kOutput, calls=%fused_computation.8 | convolution fusion | flops 1610874880 | bytes 3145729 | tf_op jit(solution)/shard_map/dot_general | solution.py:13
  12.6 0.0 all-reduce.4.cloned.1.call-update
  12.6 0.0 all-gather.2.cloned.1.call-start
  12.7 0.0 copy-done.3
  12.7 0.8 copy.6
  13.4 0.0 all-gather.2.cloned.1.call-update
  13.5 0.0 all-reduce.6.cloned.1.call-start
  13.5 69.3 %all-reduce.4.cloned.1.call-done = f32[512,512]{1,0:T(8,128)} async-done(((f32[512,512]{1,0:T(8,128)}), f32[512,512]{1,0:T(8,128)}) %all-reduce.4.cloned.1.call-update) | async-done | bytes 1048592 | tf_op jit(solution)/shard_map/psum | solution.py:9
  82.8 0.0 copy-start
  82.8 35.0 %all-gather.2.cloned.1.call-done = f32[1024,4,512]{2,0,1:T(8,128)} async-done(((f32[32,4,512]{2,0,1:T(8,128)}), f32[1024,4,512]{2,0,1:T(8,128)}) %all-gather.2.cloned.1.call-update) | async-done | bytes 8388624 | tf_op jit(solution)/shard_map/all_gather | solution.py:24
  117.8 3.7 %fusion.3 = f32[512,512]{1,0:T(8,128)S(1)} fusion(f32[512,512]{1,0:T(8,128)} %all-reduce.4.cloned.1.call-done, f32[1024,4,512]{2,0,1:T(8,128)} %all-gather.2.cloned.1.call-done, f32[4,512,512]{2,1,0:T(8,128)} %param.7), kind=kOutput, calls=%fused_computation.5 | convolution fusion | flops 1610874880 | bytes 4194304 | tf_op jit(solution)/shard_map/kr,kj->rj/dot_general | solution.py:28
  121.6 0.0 copy-done.1
  121.6 2.8 fusion.4
  124.4 0.0 all-reduce.6.cloned.1.call-update
  124.4 0.0 copy-done
  124.5 1.0 constant_dynamic-update-slice_fusion.1
  125.5 62.2 %all-reduce.6.cloned.1.call-done = f32[512,512]{1,0:T(8,128)} async-done(((f32[512,512]{1,0:T(8,128)}), f32[512,512]{1,0:T(8,128)}) %all-reduce.6.cloned.1.call-update) | async-done | bytes 1048592 | tf_op jit(solution)/shard_map/psum | solution.py:9
  187.7 2.3 constant_dynamic-update-slice_fusion
  190.0 9.7 %all-to-all-start = ((f32[32,32,512]{2,1,0:T(8,128)}), f32[32,32,512]{2,1,0:T(8,128)}, u32[]{:S(2)}, u32[]{:S(2)}) async-start(f32[32,32,512]{2,1,0:T(8,128)} %bitcast.10), calls=%async_computation | async-start | bytes 4194304 | tf_op jit(solution)/shard_map/all_to_all | solution.py:36
  199.7 0.2 all-reduce.8.cloned.1.call-start
  199.9 17.7 %bitcast_subtract_fusion = f32[4,512,512]{2,1,0:T(8,128)} fusion(f32[4,512,512]{2,1,0:T(8,128)} %param.7, f32[1024,4,512]{2,0,1:T(8,128)} %all-gather.2.cloned.1.call-done, f32[1024,512]{1,0:T(8,128)} %constant_dynamic-update-slice_fusion), kind=kOutput, calls=%fused_computation.2 | convolution fusion | flops 12885950464 | bytes 18874368 | tf_op jit(solution)/shard_map/kcr,kj->crj/dot_general | solution.py:32
  217.7 30.3 %all-to-all-done = f32[32,32,512]{2,1,0:T(8,128)} async-done(((f32[32,32,512]{2,1,0:T(8,128)}), f32[32,32,512]{2,1,0:T(8,128)}, u32[]{:S(2)}, u32[]{:S(2)}) %all-to-all-start) | async-done | bytes 2097184 | tf_op jit(solution)/shard_map/all_to_all | solution.py:36
  248.0 1.0 dynamic-slice_bitcast_fusion
  248.9 1.7 convolution_select_fusion.2
  250.6 0.0 all-reduce.8.cloned.1.call-update
  250.6 2.9 fusion.11
  253.5 59.9 %all-reduce.8.cloned.1.call-done = f32[32,512]{1,0:T(8,128)} async-done(((f32[32,512]{1,0:T(8,128)}), f32[32,512]{1,0:T(8,128)}) %all-reduce.8.cloned.1.call-update) | async-done | bytes 65552 | tf_op jit(solution)/shard_map/psum | solution.py:9
  313.4 0.0 copy-start.2
  313.4 4.7 %fusion.5 = f32[32,4,512]{2,0,1:T(8,128)S(1)} fusion(f32[32,4,512]{2,0,1:T(8,128)S(1)} %dynamic-slice_bitcast_fusion, f32[1024,4,512]{2,0,1:T(8,128)} %all-gather.2.cloned.1.call-done, f32[32,512]{1,0:T(8,128)} %all-reduce.8.cloned.1.call-done), kind=kOutput, calls=%fused_computation.9 | convolution fusion | flops 402718720 | bytes 4784128 | tf_op jit(solution)/shard_map/kn,ncr->kcr/dot_general | solution.py:42
  318.2 0.0 copy-done.2
  318.2 0.9 copy.12
  (1 shorter events, 0.0 us)
Async XLA Ops:
  8.0 4.7 %copy-start.3 = (f32[32,4,512]{2,1,0:T(4,128)S(1)}, f32[32,4,512]{2,1,0:T(4,128)}, u32[]{:S(2)}) copy-start(f32[32,4,512]{2,1,0:T(4,128)} %param.8) | copy-start | bytes 786436
  8.0 74.8 %all-reduce.4.cloned.1.call-start = ((), (), s32[]{:S(2)}) async-start(), calls=%async_computation.1 | async-start | bytes 2097152 | tf_op jit(solution)/shard_map/psum | solution.py:9
  8.1 113.5 %copy-start.1 = (f32[2,512,512]{2,1,0:T(8,128)S(1)}, f32[2,512,512]{2,1,0:T(8,128)}, u32[]{:S(2)}) copy-start(f32[2,512,512]{2,1,0:T(8,128)} %param.9) | copy-start | bytes 6291460
  12.6 105.2 %all-gather.2.cloned.1.call-start = ((), (), s32[]{:S(2)}) async-start(), calls=%async_computation.2 | async-start | bytes 8650752 | tf_op jit(solution)/shard_map/all_gather | solution.py:24
  13.5 174.2 %all-reduce.6.cloned.1.call-start = ((), (), s32[]{:S(2)}) async-start(), calls=%async_computation.3 | async-start | bytes 2097152 | tf_op jit(solution)/shard_map/psum | solution.py:9
  82.8 41.6 %copy-start = (f32[512,512]{1,0:T(8,128)S(1)}, f32[512,512]{1,0:T(8,128)}, u32[]{:S(2)}) copy-start(f32[512,512]{1,0:T(8,128)} %all-reduce.4.cloned.1.call-done) | copy-start | bytes 3145732
  190.0 57.9 %all-to-all-start = ((f32[32,32,512]{2,1,0:T(8,128)}), f32[32,32,512]{2,1,0:T(8,128)}, u32[]{:S(2)}, u32[]{:S(2)}) async-start(f32[32,32,512]{2,1,0:T(8,128)} %bitcast.10), calls=%async_computation | async-start | bytes 4194304 | tf_op jit(solution)/shard_map/all_to_all | solution.py:36
  199.7 113.7 %all-reduce.8.cloned.1.call-start = ((), (), s32[]{:S(2)}) async-start(), calls=%async_computation.4 | async-start | bytes 131072 | tf_op jit(solution)/shard_map/psum | solution.py:9
  313.4 4.7 %copy-start.2 = (f32[32,512]{1,0:T(8,128)S(1)}, f32[32,512]{1,0:T(8,128)}, u32[]{:S(2)}) copy-start(f32[32,512]{1,0:T(8,128)} %all-reduce.8.cloned.1.call-done) | copy-start | bytes 196612
Sparse Core Ops, SparseCore 0:
  12.7 70.0 all-reduce.3
  124.6 63.0 all-reduce.5
  250.8 62.6 all-reduce.7
Sparse Core Ops, SparseCore 1:
  16.2 101.5 all-gather.1
where the time goes:
time: 328 us; the launch traced here: 326 us
  waiting for transfers between devices  257 us (78%)
  matrix products  35.2 us (11%)
  between operations  15.3 us (5%)
  starting transfers between devices  10 us (3%)
  local copies, waits for them, and re-layouts  5.99 us (2%)
    psum x3, waiting for transfers between devices, broadcast(): return lax.psum(block, axis)  191 us
    all_gather x1, waiting for transfers between devices, on_device(): l_columns = lax.all_gather(l_panel, 'col', axis=0, tiled=True)  35 us
    all_to_all x1, waiting for transfers between devices, on_device(): lax.all_to_all(panels, 'col', split_axis=0, concat_axis=1, tiled=True)  30.3 us
    dot_general x1, matrix products, on_device(): jnp.einsum('kcr,kj->crj', l_columns, panels, precision=highest)  17.7 us
    all_to_all x1, starting transfers between devices, on_device(): lax.all_to_all(panels, 'col', split_axis=0, concat_axis=1, tiled=True)  9.7 us
    dot_general x3, matrix products, product(): jnp.dot(left, right_side, precision=lax.Precision.HIGHEST, preferred_elem...  9.03 us
  transfers between devices with their start and end apart: 5, of which 5 were waited for; matrix products, arithmetic and copies ran while one was open for 7% of the time, Pallas kernels for 0%

commit v1 on v0

v1 whole, which is shorter than its diff:
```python
import jax
import jax.numpy as jnp
from jax import lax
from jax.experimental import pallas as pl
from jax.experimental.pallas import tpu as pltpu
from jax.sharding import PartitionSpec as P

ROWS, Y, Z = 8, 4, 8
COLS = Y * Z
HIGH = lax.Precision.HIGH
Y_ORDER = (0, 1, -1, -2)
Z_ORDER = (0, 1, -1, -2, 2, 3, -3, -4)


def flat(r, y, z):
    return r * COLS + (y % Y) * Z + z % Z


def permute(x, pairs):
    return lax.ppermute(x, ("row", "col"), pairs)


def neighbour_pairs(axis, step):
    pairs = []
    for r in range(ROWS):
        for y in range(Y):
            for z in range(Z):
                at = y if axis == "y" else z
                side = 1 if ((at + r) % 2 == 0) == (step % 2 == 1) else -1
                to = flat(r, y + side, z) if axis == "y" else flat(r, y, z + side)
                pairs.append((flat(r, y, z), to))
    return pairs


def ring_gather(x, axis):
    size = Y if axis == "y" else Z
    got = permute(x, neighbour_pairs(axis, 1))
    blocks = [x, got]
    held = jnp.concatenate(blocks, axis=0)
    for step in range(2, size // 2 + 1):
        held = permute(held, neighbour_pairs(axis, step))
        blocks.append(held)
    return jnp.concatenate(blocks, axis=0)


def to_other_chips(x):
    row = lax.axis_index("row")
    chip = row // 2
    mine = x
    for j in (1, 3, 2):
        got = lax.ppermute(x, "row", [(0, 2 * j), (1, 2 * j + 1)])
        mine = jnp.where(chip == j, got, mine)
    return mine


def swap_cores(x):
    return lax.ppermute(x, "row", [(r, r ^ 1) for r in range(ROWS)])


def reorder_kernel(index_ref, x_ref, o_ref):
    def body(i, carry):
        o_ref[pl.ds(pl.multiple_of(i * 16, 16), 16), :] = x_ref[
            pl.ds(pl.multiple_of(index_ref[i] * 16, 16), 16), :
        ]
        return carry

    lax.fori_loop(0, index_ref.shape[0], body, 0)


def reorder(x, index):
    return pl.pallas_call(
        reorder_kernel,
        out_shape=jax.ShapeDtypeStruct(x.shape, x.dtype),
        grid_spec=pltpu.PrefetchScalarGridSpec(
            num_scalar_prefetch=1,
            grid=(1,),
            in_specs=[pl.BlockSpec(x.shape, lambda i, s: (0, 0))],
            out_specs=pl.BlockSpec(x.shape, lambda i, s: (0, 0)),
        ),
        compiler_params=pltpu.CompilerParams(vmem_limit_bytes=24 * 2**20),
    )(index, x)


def product(left, right_side):
    return jnp.dot(left, right_side, precision=HIGH, preferred_element_type=jnp.float32)


def from_left(left, right_side):
    return lax.dot_general(
        left,
        right_side,
        (((0,), (0,)), ((), ())),
        precision=HIGH,
        preferred_element_type=jnp.float32,
    )


def on_device(a_block, l_panel, inverses):
    row, col = lax.axis_index("row"), lax.axis_index("col")
    core, chip, y, z = row % 2, row // 2, col // Z, col % Z

    piece = l_panel[:, 0, :]
    piece = to_other_chips(piece)
    other = swap_cores(piece)
    piece = jnp.where(core == 1, piece, other)
    swapped = permute(piece, [(flat(r, i, k), flat(r, i ^ 1, k)) for r in range(ROWS) for i in range(Y) for k in range(Z)])
    pair = jnp.stack([jnp.where(y == 0, piece, swapped), jnp.where(y == 0, swapped, piece)])
    sent = permute(pair, [(flat(r, i, k), flat(r, 3 - i, k)) for r in range(ROWS) for i in range(Y) for k in range(Z)])
    pair = jnp.where(y < 2, pair, sent)
    gathered = ring_gather(pair[None], "z")
    z_side = jnp.where((z + core) % 2 == 0, 1, -1)
    y_side = jnp.where((y + core) % 2 == 0, 1, -1)
    z_list = (z + z_side * jnp.array(Z_ORDER, jnp.int32)) % Z
    y_list = (y + y_side * jnp.array(Y_ORDER, jnp.int32)) % Y

    tile = to_other_chips(a_block[0])
    other = swap_cores(tile)
    first_rows = jnp.where(core == 0, tile, other)
    second_rows = jnp.where(core == 0, other, tile)

    shard = l_panel.reshape(32, 2048)
    l_a = ring_gather(ring_gather(shard[:16], "y"), "z")
    l_b = ring_gather(ring_gather(shard[16:], "z"), "y")

    w_first = product(inverses[0], first_rows)
    w_blocks = w_first.reshape(2, Z, 32, 512).transpose(1, 0, 2, 3).reshape(Z * 4, 16, 512)
    z_index = (z_list[:, None] * 4 + jnp.arange(4, dtype=jnp.int32)[None, :]).reshape(-1)
    w_ordered = reorder(w_blocks.reshape(512, 512), z_index)
    coupling = from_left(gathered.reshape(512, 512), w_ordered)
    w_second = product(inverses[1], second_rows - coupling)
    panels = jnp.concatenate([w_first, w_second], axis=0)

    block_of = lambda yy, zz, half: (yy * Z + zz) * 2 + half
    order = jnp.concatenate([
        block_of(y_list[None, :], z_list[:, None], 0).reshape(-1),
        block_of(y_list[:, None], z_list[None, :], 1).reshape(-1),
    ])

    pieces = panels.reshape(COLS, 2, 16, 4, 128)
    pieces = lax.dynamic_index_in_dim(pieces, core, 1, keepdims=False)
    pieces = lax.dynamic_index_in_dim(pieces, chip, 2, keepdims=False)
    pieces = lax.all_to_all(pieces, "col", 0, 0, tiled=True).reshape(Y, Z, 16, 128)
    first_tile = jnp.broadcast_to(pieces[0, 0], (ROWS, 1, 16, 128))
    pieces = jnp.concatenate([pieces.transpose(1, 0, 2, 3), first_tile], axis=1)
    pieces = lax.all_to_all(pieces, "row", 0, 0, tiled=True).reshape(4, 2, Y + 1, 16, 128)
    own = pieces.transpose(2, 1, 3, 0, 4).reshape(Y + 1, 32, 512)

    panels_ordered = reorder(panels, order)
    remaining = a_block.reshape(2048, 512) - from_left(l_a, panels_ordered[:512]) - from_left(l_b, panels_ordered[512:])
    remaining = remaining.reshape(4, 512, 512)
    top = jnp.where(row == 0, w_first, jnp.where(row == 1, w_second, remaining[0]))
    reduced = remaining.at[0].set(top)

    y_first = lax.dot_general(inverses[0], own[Y], (((1,), (1,)), ((), ())), precision=HIGH, preferred_element_type=jnp.float32)
    y_all = jnp.concatenate([y_first, jnp.zeros_like(y_first)], axis=0)
    y_ordered = reorder(y_all, order)
    solved = from_left(y_ordered[:512], l_a) + from_left(y_ordered[512:], l_b)
    right_out = own[:Y].transpose(1, 0, 2) - solved.reshape(32, 4, 512)
    right_out = right_out.at[:, 0, :].set(jnp.where(row == 0, y_first.T, right_out[:, 0, :]))
    return (reduced, right_out)


def solution(mesh):
    return jax.shard_map(
        on_device,
        mesh=mesh,
        in_specs=(P(None, "row", "col"), P("col", None, "row"), P()),
        out_specs=(P(None, "row", "col"), P("col", None, "row")),
        check_vma=False,
    )
```

time: 328 us -> 165 us (0.50)
  waiting for transfers between devices: 257 us -> 31.2 us
  starting transfers between devices: 10 us -> 63 us
  local copies, waits for them, and re-layouts: 5.99 us -> 40.1 us
  matrix products: 35.2 us -> 18.6 us
  between operations: 15.3 us -> 1.15 us
  other arithmetic: 2.88 us -> 6.41 us
    psum x3 -> x0, waiting for transfers between devices: 191 us -> none  [broadcast(): return lax.psum(block, axis)]
    ppermute x0 -> x26, starting transfers between devices: none -> 45.3 us  [the longest x18 23.2 us: permute(): return lax.ppermute(x, ('row', 'col'), pairs)]
    all_gather x1 -> x0, waiting for transfers between devices: 35 us -> none  [on_device(): l_columns = lax.all_gather(l_panel, 'col', axis=0, tiled=True)]
    ppermute x0 -> x26, waiting for transfers between devices: none -> 24.8 us  [the longest x18 23.7 us: permute(): return lax.ppermute(x, ('row', 'col'), pairs)]
    all_to_all x1 -> x2, waiting for transfers between devices: 30.3 us -> 6.36 us  [the longest x1 5.83 us: on_device(): lax.all_to_all(pieces, 'col', 0, 0, tiled=True).reshape(Y, Z, 16, 128)]
    unnamed x11 -> x53, local copies, waits for them, and re-layouts: 2.72 us -> 23.7 us
    dot_general x6 -> x8, matrix products: 35.2 us -> 18.6 us  [the longest x5 13.5 us: from_left(): lax.dot_general(left, right_side, (((0,), (0,)), ((), ())), precision=HIG...]
    all_to_all x1 -> x2, starting transfers between devices: 9.7 us -> 17.7 us  [the longest x1 9.45 us: on_device(): lax.all_to_all(pieces, 'row', 0, 0, tiled=True)]
  transfers between devices with their start and end apart: 5 -> 28, of which waited for: 5 -> 13; matrix products, arithmetic and copies ran while one was open for 7% -> 29% of each run, Pallas kernels for 0% -> 2%
where the time goes in v1:
time: 165 us; the launch traced here: 163 us
  starting transfers between devices  63 us (38%)
  local copies, waits for them, and re-layouts  40.1 us (24%)
  waiting for transfers between devices  31.2 us (19%)
  matrix products  18.6 us (11%)
  other arithmetic  6.41 us (4%)
  Pallas kernels  2.75 us (2%)
    unnamed x53, local copies, waits for them, and re-layouts  23.7 us
    ppermute x18, waiting for transfers between devices, permute(): return lax.ppermute(x, ('row', 'col'), pairs)  23.7 us
    ppermute x18, starting transfers between devices, permute(): return lax.ppermute(x, ('row', 'col'), pairs)  23.2 us
    ppermute x6, starting transfers between devices, to_other_chips(): got = lax.ppermute(x, 'row', [(0, 2 * j), (1, 2 * j + 1)])  14 us
    dot_general x5, matrix products, from_left(): lax.dot_general(left, right_side, (((0,), (0,)), ((), ())), precision=HIG...  13.5 us
    all_to_all x1, starting transfers between devices, on_device(): lax.all_to_all(pieces, 'row', 0, 0, tiled=True)  9.45 us
    all_to_all x1, starting transfers between devices, on_device(): lax.all_to_all(pieces, 'col', 0, 0, tiled=True).reshape(Y, Z, 16, 128)  8.23 us
    ppermute x2, starting transfers between devices, swap_cores(): return lax.ppermute(x, 'row', [(r, r ^ 1) for r in range(ROWS)])  8.2 us
  transfers between devices with their start and end apart: 28, of which 13 were waited for; matrix products, arithmetic and copies ran while one was open for 29% of the time, Pallas kernels for 2%

profile of v1, /device:TPU:1, one launch (start us, length us, event | category | flops | bytes accessed | tf_op | source)
XLA Modules:
  0.0 163.2 jit_solution(2790819991216593186)
XLA Ops:
  1.7 5.5 %collective-permute-start.10 = (f32[32,512]{1,0:T(8,128)S(1)}, f32[32,512]{1,0:T(8,128)S(1)}, u32[]{:S(2)}, u32[]{:S(2)}) collective-permute-start(f32[32,512]{1,0:T(8,128)S(1)} %bitcast.107), channel_id=1, source_target_pairs={{0,128},{32,160},{1,129},{33,161},{2,130},{34,162},{3,131},{35,163... | collective-permute-start | bytes 196616 | tf_op jit(solution)/shard_map/ppermute | solution.py:51
  7.2 1.3 collective-permute-start.11
  8.5 1.3 collective-permute-start.12
  9.8 1.3 slice_bitcast_fusion
  11.1 1.4 collective-permute-start.6
  12.4 2.3 %collective-permute-start.7 = (f32[512,512]{1,0:T(8,128)S(1)}, f32[512,512]{1,0:T(8,128)}, u32[]{:S(2)}, u32[]{:S(2)}) collective-permute-start(f32[512,512]{1,0:T(8,128)S(1)} %slice_bitcast_fusion), channel_id=1, source_target_pairs={{0,192},{32,224},{1,193},{33,225},{2,194},{34,226},{3,195},{35,227... | collective-permute-start | bytes 3145736 | tf_op jit(solution)/shard_map/ppermute | solution.py:51
  17.4 2.3 %collective-permute-start.8 = (f32[512,512]{1,0:T(8,128)S(1)}, f32[512,512]{1,0:T(8,128)}, u32[]{:S(2)}, u32[]{:S(2)}) collective-permute-start(f32[512,512]{1,0:T(8,128)S(1)} %slice_bitcast_fusion), channel_id=1, source_target_pairs={{0,64},{32,96},{1,65},{33,97},{2,66},{34,98},{3,67},{35,99},{4,68}... | collective-permute-start | bytes 3145736 | tf_op jit(solution)/shard_map/ppermute | solution.py:51
  19.7 5.6 %collective-permute-start.20 = (f32[16,2048]{1,0:T(8,128)S(1)}, f32[16,2048]{1,0:T(8,128)S(1)}, u32[]{:S(2)}, u32[]{:S(2)}) collective-permute-start(f32[16,2048]{1,0:T(8,128)S(1)} %bitcast.99), channel_id=1, source_target_pairs={{0,1},{1,0},{2,3},{3,2},{4,5},{5,4},{6,7},{7,6},{8,9},{9,8},{10,11... | collective-permute-start | bytes 393224 | tf_op jit(solution)/shard_map/ppermute | solution.py:20
  25.5 1.2 collective-permute-done.13
  26.6 2.7 %collective-permute-start = (f32[16,2048]{1,0:T(8,128)S(1)}, f32[16,2048]{1,0:T(8,128)S(1)}, u32[]{:S(2)}, u32[]{:S(2)}) collective-permute-start(f32[16,2048]{1,0:T(8,128)S(1)} %bitcast.91), channel_id=1, source_target_pairs={{0,8},{1,9},{2,10},{3,11},{4,12},{5,13},{6,14},{7,15},{8,0},{9,1},... | collective-permute-start | bytes 393224 | tf_op jit(solution)/shard_map/ppermute | solution.py:20
  30.3 2.5 %collective-permute-done.14 = f32[32,512]{1,0:T(8,128)S(1)} collective-permute-done((f32[32,512]{1,0:T(8,128)S(1)}, f32[32,512]{1,0:T(8,128)S(1)}, u32[]{:S(2)}, u32[]{:S(2)}) %collective-permute-start.14) | collective-permute-done | bytes 65568 | tf_op jit(solution)/shard_map/ppermute | solution.py:20
  32.8 1.7 %collective-permute-start.15 = (f32[2,32,512]{2,1,0:T(8,128)S(1)}, f32[2,32,512]{2,1,0:T(8,128)S(1)}, u32[]{:S(2)}, u32[]{:S(2)}) collective-permute-start(f32[2,32,512]{2,1,0:T(8,128)S(1)} %pad_maximum_fusion.7), channel_id=1, source_target_pairs={{0,24},{1,25},{2,26},{3,27},{4,28},{5,29},{6,30},{7,31},{8,16},{9,... | collective-permute-start | bytes 393224 | tf_op jit(solution)/shard_map/ppermute | solution.py:20
  34.5 4.5 %collective-permute-done.15 = f32[2,32,512]{2,1,0:T(8,128)S(1)} collective-permute-done((f32[2,32,512]{2,1,0:T(8,128)S(1)}, f32[2,32,512]{2,1,0:T(8,128)S(1)}, u32[]{:S(2)}, u32[]{:S(2)}) %collective-permute-start.15) | collective-permute-done | bytes 131104 | tf_op jit(solution)/shard_map/ppermute | solution.py:20
  39.7 2.0 %collective-permute-start.16 = (f32[1,2,32,512]{3,2,1,0:T(8,128)S(1)}, f32[1,2,32,512]{3,2,1,0:T(8,128)S(1)}, u32[]{:S(2)}, u32[]{:S(2)}) collective-permute-start(f32[1,2,32,512]{3,2,1,0:T(8,128)S(1)} %get-tuple-element.37), channel_id=1, source_target_pairs={{0,1},{1,0},{2,3},{3,2},{4,5},{5,4},{6,7},{7,6},{8,9},{9,8},{10,11... | collective-permute-start | bytes 393224 | tf_op jit(solution)/shard_map/ppermute | solution.py:20
  41.7 2.8 %collective-permute-done.21 = f32[32,2048]{1,0:T(8,128)S(1)} collective-permute-done((f32[32,2048]{1,0:T(8,128)S(1)}, f32[32,2048]{1,0:T(8,128)S(1)}, u32[]{:S(2)}, u32[]{:S(2)}) %collective-permute-start.21) | collective-permute-done | bytes 262176 | tf_op jit(solution)/shard_map/ppermute | solution.py:20
  44.5 1.2 collective-permute-done.16
  45.7 2.0 %collective-permute-start.22 = (f32[32,2048]{1,0:T(8,128)S(1)}, f32[32,2048]{1,0:T(8,128)S(1)}, u32[]{:S(2)}, u32[]{:S(2)}) collective-permute-start(f32[32,2048]{1,0:T(8,128)S(1)} %collective-permute-done.21), channel_id=1, source_target_pairs={{0,1},{1,0},{2,3},{3,2},{4,5},{5,4},{6,7},{7,6},{8,9},{9,8},{10,11... | collective-permute-start | bytes 786440 | tf_op jit(solution)/shard_map/ppermute | solution.py:20
  49.7 2.4 %collective-permute-done.22 = f32[32,2048]{1,0:T(8,128)S(1)} collective-permute-done((f32[32,2048]{1,0:T(8,128)S(1)}, f32[32,2048]{1,0:T(8,128)S(1)}, u32[]{:S(2)}, u32[]{:S(2)}) %collective-permute-start.22) | collective-permute-done | bytes 262176 | tf_op jit(solution)/shard_map/ppermute | solution.py:20
  53.9 3.2 %collective-permute-done.17 = f32[2,2,32,512]{3,2,1,0:T(8,128)} collective-permute-done((f32[2,2,32,512]{3,2,1,0:T(8,128)S(1)}, f32[2,2,32,512]{3,2,1,0:T(8,128)}, u32[]{:S(2)}, u32[]{:S(2)}) %collective-permute-start.17) | collective-permute-done | bytes 262176 | tf_op jit(solution)/shard_map/ppermute | solution.py:20
  57.1 3.8 %collective-permute-done.23 = f32[32,2048]{1,0:T(8,128)S(1)} collective-permute-done((f32[32,2048]{1,0:T(8,128)S(1)}, f32[32,2048]{1,0:T(8,128)S(1)}, u32[]{:S(2)}, u32[]{:S(2)}) %collective-permute-start.23) | collective-permute-done | bytes 262176 | tf_op jit(solution)/shard_map/ppermute | solution.py:20
  62.4 1.2 collective-permute-start.24
  63.7 1.8 %select_select_fusion = f32[512,512]{1,0:T(8,128)S(1)} fusion(f32[512,512]{1,0:T(8,128)S(1)} %collective-permute-done.6, f32[512,512]{1,0:T(8,128)} %collective-permute-done.7, f32[512,512]{1,0:T(8,128)} %collective-permute-done.8, pred[]{:T(512)S(6)} %eq.50, pred[]{:T(512)S(6)} %eq.49, pred[]{:T(512)S(6)} %eq.48, f32[4,512,512]{2,1,0:T(8,128)} %param.9), kind=kLoop, calls=%fused_computation.21 | loop fusion | flops 786432 | bytes 5242883 | tf_op jit(solution)/shard_map/jit(_where)/select_n | solution.py:52
  65.5 8.1 %collective-permute-start.9 = (f32[512,512]{1,0:T(8,128)S(1)}, f32[512,512]{1,0:T(8,128)S(1)}, u32[]{:S(2)}, u32[]{:S(2)}) collective-permute-start(f32[512,512]{1,0:T(8,128)S(1)} %select_select_fusion), channel_id=1, source_target_pairs={{0,32},{32,0},{64,96},{96,64},{128,160},{160,128},{192,224},{224,1... | collective-permute-start | bytes 3145736 | tf_op jit(solution)/shard_map/ppermute | solution.py:57
  74.6 1.7 %constant_dynamic-update-slice_fusion.9 = f32[8,2,32,512]{3,2,1,0:T(8,128)} fusion(f32[8,2,32,512]{3,2,1,0:T(8,128)} %constant_dynamic-update-slice_fusion.10, f32[2,2,32,512]{3,2,1,0:T(8,128)} %collective-permute-done.17), kind=kLoop, calls=%fused_computation.56 | loop fusion | bytes 524288
  76.3 1.7 %collective-permute-start.19 = (f32[2,2,32,512]{3,2,1,0:T(8,128)}, f32[2,2,32,512]{3,2,1,0:T(8,128)S(1)}, u32[]{:S(2)}, u32[]{:S(2)}) collective-permute-start(f32[2,2,32,512]{3,2,1,0:T(8,128)} %collective-permute-done.18), channel_id=1, source_target_pairs={{0,7},{1,2},{2,1},{3,4},{4,3},{5,6},{6,5},{7,0},{8,15},{9,10},{10,... | collective-permute-start | bytes 786440 | tf_op jit(solution)/shard_map/ppermute | solution.py:20
  79.2 1.7 %constant_dynamic-update-slice_fusion.8 = f32[8,2,32,512]{3,2,1,0:T(8,128)} fusion(f32[8,2,32,512]{3,2,1,0:T(8,128)} %constant_dynamic-update-slice_fusion.9, f32[2,2,32,512]{3,2,1,0:T(8,128)} %collective-permute-done.18), kind=kLoop, calls=%fused_computation.55 | loop fusion | bytes 524288
  80.8 1.6 collective-permute-done.19
  83.2 2.8 %constant_dynamic-update-slice_fusion.17 = (f32[256,2048]{1,0:T(8,128)}, f32[512,2048]{1,0:T(8,128)}) fusion(f32[256,2048]{1,0:T(8,128)} %get-tuple-element.42, f32[128,2048]{1,0:T(8,128)} %collective-permute-done.24, f32[512,2048]{1,0:T(8,128)} %get-tuple-element.43), kind=kLoop, calls=%fused_computation.64 | loop fusion | bytes 3145728 | tf_op jit(solution)/shard_map/concatenate | solution.py:39
  85.9 1.7 %collective-permute-start.25 = (f32[256,2048]{1,0:T(8,128)}, f32[256,2048]{1,0:T(8,128)}, u32[]{:S(2)}, u32[]{:S(2)}) collective-permute-start(f32[256,2048]{1,0:T(8,128)} %get-tuple-element.38), channel_id=1, source_target_pairs={{0,24},{1,25},{2,26},{3,27},{4,28},{5,29},{6,30},{7,31},{8,16},{9,... | collective-permute-start | bytes 6291464 | tf_op jit(solution)/shard_map/ppermute | solution.py:20
  87.7 2.2 %fusion.10 = f32[512,512]{0,1:T(8,128)S(1)} fusion(f32[512,512]{1,0:T(8,128)S(1)} %select_select_fusion, f32[512,512]{1,0:T(8,128)S(1)} %collective-permute-done.9, f32[2,512,512]{2,1,0:T(8,128)} %param.11, pred[]{:T(512)S(6)} %eq.47), kind=kOutput, calls=%fused_computation.17 | convolution fusion | flops 805568512 | bytes 4194305 | tf_op jit(solution)/shard_map/dot_general | solution.py:85
  94.1 1.8 %reshape.133 = f32[32,2,16,4,128]{4,3,2,1,0:T(4,128)} reshape(f32[1024,512]{1,0:T(8,128)S(1)} %pad_maximum_fusion.x_ref) | data formatting | bytes 4194304 | tf_op jit(solution)/shard_map/reshape | solution.py:139
  95.9 2.2 %constant_dynamic-slice_fusion = f32[32,1,16,1,128]{4,3,2,1,0:T(1,128)} fusion(f32[32,2,16,4,128]{4,3,2,1,0:T(4,128)} %reshape.133, s32[]{:T(128)S(6)} %select_n.188, s32[]{:T(128)S(6)} %select_n.190), kind=kLoop, calls=%fused_computation.88 | loop fusion | bytes 524296 | tf_op jit(solution)/shard_map/jit(dynamic_index_in_dim)/dynamic_slice | solution.py:141
  98.1 8.2 %all-to-all-start = ((f32[32,16,128]{2,1,0:T(8,128)}), f32[32,16,128]{2,1,0:T(8,128)}, u32[]{:S(2)}, u32[]{:S(2)}) async-start(f32[32,16,128]{2,1,0:T(8,128)} %bitcast.102), calls=%async_computation | async-start | bytes 524288 | tf_op jit(solution)/shard_map/all_to_all | solution.py:142
  107.1 2.4 %collective-permute-start.4 = (f32[128,2048]{1,0:T(8,128)}, f32[128,2048]{1,0:T(8,128)}, u32[]{:S(2)}, u32[]{:S(2)}) collective-permute-start(f32[128,2048]{1,0:T(8,128)} %collective-permute-done.3), channel_id=1, source_target_pairs={{0,1},{1,0},{2,3},{3,2},{4,5},{5,4},{6,7},{7,6},{8,9},{9,8},{10,11... | collective-permute-start | bytes 3145736 | tf_op jit(solution)/shard_map/ppermute | solution.py:20
  110.2 5.8 %all-to-all-done = f32[32,16,128]{2,1,0:T(8,128)} async-done(((f32[32,16,128]{2,1,0:T(8,128)}), f32[32,16,128]{2,1,0:T(8,128)}, u32[]{:S(2)}, u32[]{:S(2)}) %all-to-all-start) | async-done | bytes 262176 | tf_op jit(solution)/shard_map/all_to_all | solution.py:142
  118.5 9.5 %all-to-all-start.1 = ((f32[8,5,16,128]{3,2,1,0:T(8,128)}), f32[8,5,16,128]{3,2,1,0:T(8,128)S(1)}, u32[]{:S(2)}, u32[]{:S(2)}) async-start(f32[8,5,16,128]{3,2,1,0:T(8,128)} %copy.26), calls=%async_computation.1 | async-start | bytes 655360 | tf_op jit(solution)/shard_map/all_to_all | solution.py:145
  127.9 1.9 %constant_dynamic-update-slice_fusion.3 = f32[512,2048]{1,0:T(8,128)} fusion(f32[512,2048]{1,0:T(8,128)} %constant_dynamic-update-slice_fusion.4, f32[64,2048]{1,0:T(8,128)} %copy-done.9), kind=kLoop, calls=%fused_computation.50 | loop fusion | bytes 1048576
  129.8 2.3 %constant_dynamic-update-slice_fusion.2 = f32[512,2048]{1,0:T(8,128)} fusion(f32[512,2048]{1,0:T(8,128)} %constant_dynamic-update-slice_fusion.3, f32[128,2048]{1,0:T(8,128)} %collective-permute-done.3), kind=kLoop, calls=%fused_computation.49 | loop fusion | bytes 2097152
  133.2 1.4 copy-done
  135.2 1.5 collective-permute-start.5
  136.6 1.8 %fusion.8 = f32[32,512]{1,0:T(8,128)S(1)} fusion(f32[2,512,512]{2,1,0:T(8,128)} %param.11, f32[4,8,4,128]{3,2,1,0:T(4,128)S(1)} %bitcast.106), kind=kOutput, calls=%fused_computation.15 | convolution fusion | flops 50331648 | bytes 1179648 | tf_op jit(solution)/shard_map/dot_general | solution.py:154
  139.8 2.3 %constant_dynamic-update-slice_fusion.1 = f32[512,2048]{1,0:T(8,128)} fusion(f32[512,2048]{1,0:T(8,128)} %constant_dynamic-update-slice_fusion.2, f32[128,2048]{1,0:T(8,128)} %collective-permute-done.4), kind=kLoop, calls=%fused_computation.48 | loop fusion | bytes 2097152
  142.1 3.3 %constant_dynamic-update-slice_fusion.23 = f32[512,2048]{1,0:T(8,128)} fusion(f32[512,2048]{1,0:T(8,128)} %get-tuple-element.39, f32[256,2048]{1,0:T(8,128)} %collective-permute-done.25), kind=kLoop, calls=%fused_computation.70 | loop fusion | bytes 4194304 | tf_op jit(solution)/shard_map/concatenate | solution.py:43
  145.4 3.6 %fusion.17 = f32[32,2048]{1,0:T(8,128)S(1)} fusion(f32[512,2048]{1,0:T(8,128)} %constant_dynamic-update-slice_fusion.23, f32[1024,32]{1,0:T(8,128)S(1)} %shard_map.70), kind=kOutput, calls=%fused_computation.29 | convolution fusion | flops 201326592 | bytes 4718592 | tf_op jit(solution)/shard_map/dot_general | solution.py:89
  149.7 1.6 convolution_add_fusion
  152.2 3.7 %fusion.4 = f32[2048,512]{1,0:T(8,128)S(1)} fusion(f32[512,2048]{1,0:T(8,128)S(1)} %copy-done.3, f32[1024,512]{1,0:T(8,128)S(1)} %copy-done.1), kind=kOutput, calls=%fused_computation.10 | convolution fusion | flops 3221225472 | bytes 9437184 | tf_op jit(solution)/shard_map/dot_general | solution.py:89
  156.0 3.7 %fusion = f32[2048,512]{1,0:T(8,128)S(1)} fusion(f32[2048,512]{1,0:T(8,128)S(1)} %fusion.4, f32[4,512,512]{2,1,0:T(8,128)S(1)} %copy-done.4, f32[512,2048]{1,0:T(8,128)S(1)} %constant_dynamic-update-slice_fusion, f32[1024,512]{1,0:T(8,128)S(1)} %copy-done.1), kind=kOutput, calls=%fused_computation.1 | convolution fusion | flops 3223322624 | bytes 17825792 | tf_op jit(solution)/shard_map/dot_general | solution.py:89
  161.2 2.0 %copy-done.8 = f32[4,512,512]{2,1,0:T(8,128)} copy-done((f32[4,512,512]{2,1,0:T(8,128)}, f32[4,512,512]{2,1,0:T(8,128)S(1)}, u32[]{:S(2)}) %copy-start.8) | copy-done | bytes 4194328
  (117 shorter events, 28.0 us)
Async XLA Ops:
  0.6 16.6 %copy-start.15 = (s32[8]{0:T(128)S(1)}, s32[8]{0:T(128)}, u32[]{:S(2)}) copy-start(s32[8]{0:T(128)} %constant.184.clone) | copy-start | bytes 100
  0.6 16.6 %copy-start.16 = (s32[4]{0:T(128)S(1)}, s32[4]{0:T(128)}, u32[]{:S(2)}) copy-start(s32[4]{0:T(128)} %constant.185.clone) | copy-start | bytes 52
  1.7 15.7 %collective-permute-start.10 = (f32[32,512]{1,0:T(8,128)S(1)}, f32[32,512]{1,0:T(8,128)S(1)}, u32[]{:S(2)}, u32[]{:S(2)}) collective-permute-start(f32[32,512]{1,0:T(8,128)S(1)} %bitcast.107), channel_id=1, source_target_pairs={{0,128},{32,160},{1,129},{33,161},{2,130},{34,162},{3,131},{35,163... | collective-permute-start | bytes 196616 | tf_op jit(solution)/shard_map/ppermute | solution.py:51
  7.2 12.5 %collective-permute-start.11 = (f32[32,512]{1,0:T(8,128)S(1)}, f32[32,512]{1,0:T(8,128)S(1)}, u32[]{:S(2)}, u32[]{:S(2)}) collective-permute-start(f32[32,512]{1,0:T(8,128)S(1)} %bitcast.108), channel_id=1, source_target_pairs={{0,192},{32,224},{1,193},{33,225},{2,194},{34,226},{3,195},{35,227... | collective-permute-start | bytes 196616 | tf_op jit(solution)/shard_map/ppermute | solution.py:51
  8.5 16.8 %collective-permute-start.12 = (f32[32,512]{1,0:T(8,128)S(1)}, f32[32,512]{1,0:T(8,128)S(1)}, u32[]{:S(2)}, u32[]{:S(2)}) collective-permute-start(f32[32,512]{1,0:T(8,128)S(1)} %bitcast.109), channel_id=1, source_target_pairs={{0,64},{32,96},{1,65},{33,97},{2,66},{34,98},{3,67},{35,99},{4,68}... | collective-permute-start | bytes 196616 | tf_op jit(solution)/shard_map/ppermute | solution.py:51
  11.1 51.4 %collective-permute-start.6 = (f32[512,512]{1,0:T(8,128)S(1)}, f32[512,512]{1,0:T(8,128)S(1)}, u32[]{:S(2)}, u32[]{:S(2)}) collective-permute-start(f32[512,512]{1,0:T(8,128)S(1)} %slice_bitcast_fusion), channel_id=1, source_target_pairs={{0,128},{32,160},{1,129},{33,161},{2,130},{34,162},{3,131},{35,163... | collective-permute-start | bytes 3145736 | tf_op jit(solution)/shard_map/ppermute | solution.py:51
  12.4 51.3 %collective-permute-start.7 = (f32[512,512]{1,0:T(8,128)S(1)}, f32[512,512]{1,0:T(8,128)}, u32[]{:S(2)}, u32[]{:S(2)}) collective-permute-start(f32[512,512]{1,0:T(8,128)S(1)} %slice_bitcast_fusion), channel_id=1, source_target_pairs={{0,192},{32,224},{1,193},{33,225},{2,194},{34,226},{3,195},{35,227... | collective-permute-start | bytes 3145736 | tf_op jit(solution)/shard_map/ppermute | solution.py:51
  17.3 8.1 %copy-start.13 = (s32[4]{0:T(128)}, s32[4]{0:T(128)S(1)}, u32[]{:S(2)}) copy-start(s32[4]{0:T(128)S(1)} %fusion.25) | copy-start | bytes 52
  17.4 46.3 %collective-permute-start.8 = (f32[512,512]{1,0:T(8,128)S(1)}, f32[512,512]{1,0:T(8,128)}, u32[]{:S(2)}, u32[]{:S(2)}) collective-permute-start(f32[512,512]{1,0:T(8,128)S(1)} %slice_bitcast_fusion), channel_id=1, source_target_pairs={{0,64},{32,96},{1,65},{33,97},{2,66},{34,98},{3,67},{35,99},{4,68}... | collective-permute-start | bytes 3145736 | tf_op jit(solution)/shard_map/ppermute | solution.py:51
  19.7 9.7 %collective-permute-start.20 = (f32[16,2048]{1,0:T(8,128)S(1)}, f32[16,2048]{1,0:T(8,128)S(1)}, u32[]{:S(2)}, u32[]{:S(2)}) collective-permute-start(f32[16,2048]{1,0:T(8,128)S(1)} %bitcast.99), channel_id=1, source_target_pairs={{0,1},{1,0},{2,3},{3,2},{4,5},{5,4},{6,7},{7,6},{8,9},{9,8},{10,11... | collective-permute-start | bytes 393224 | tf_op jit(solution)/shard_map/ppermute | solution.py:20
  25.3 1.3 collective-permute-start.13
  26.6 13.1 %collective-permute-start = (f32[16,2048]{1,0:T(8,128)S(1)}, f32[16,2048]{1,0:T(8,128)S(1)}, u32[]{:S(2)}, u32[]{:S(2)}) collective-permute-start(f32[16,2048]{1,0:T(8,128)S(1)} %bitcast.91), channel_id=1, source_target_pairs={{0,8},{1,9},{2,10},{3,11},{4,12},{5,13},{6,14},{7,15},{8,0},{9,1},... | collective-permute-start | bytes 393224 | tf_op jit(solution)/shard_map/ppermute | solution.py:20
  29.4 3.4 %collective-permute-start.14 = (f32[32,512]{1,0:T(8,128)S(1)}, f32[32,512]{1,0:T(8,128)S(1)}, u32[]{:S(2)}, u32[]{:S(2)}) collective-permute-start(f32[32,512]{1,0:T(8,128)S(1)} %broadcast_select_fusion), channel_id=1, source_target_pairs={{0,8},{1,9},{2,10},{3,11},{4,12},{5,13},{6,14},{7,15},{8,0},{9,1},... | collective-permute-start | bytes 196616 | tf_op jit(solution)/shard_map/ppermute | solution.py:20
  32.8 6.2 %collective-permute-start.15 = (f32[2,32,512]{2,1,0:T(8,128)S(1)}, f32[2,32,512]{2,1,0:T(8,128)S(1)}, u32[]{:S(2)}, u32[]{:S(2)}) collective-permute-start(f32[2,32,512]{2,1,0:T(8,128)S(1)} %pad_maximum_fusion.7), channel_id=1, source_target_pairs={{0,24},{1,25},{2,26},{3,27},{4,28},{5,29},{6,30},{7,31},{8,16},{9,... | collective-permute-start | bytes 393224 | tf_op jit(solution)/shard_map/ppermute | solution.py:20
  39.0 5.5 %collective-permute-start.21 = (f32[32,2048]{1,0:T(8,128)S(1)}, f32[32,2048]{1,0:T(8,128)S(1)}, u32[]{:S(2)}, u32[]{:S(2)}) collective-permute-start(f32[32,2048]{1,0:T(8,128)S(1)} %pad_maximum_fusion.6), channel_id=1, source_target_pairs={{0,7},{1,2},{2,1},{3,4},{4,3},{5,6},{6,5},{7,0},{8,15},{9,10},{10,... | collective-permute-start | bytes 786440 | tf_op jit(solution)/shard_map/ppermute | solution.py:20
  39.7 6.0 %collective-permute-start.16 = (f32[1,2,32,512]{3,2,1,0:T(8,128)S(1)}, f32[1,2,32,512]{3,2,1,0:T(8,128)S(1)}, u32[]{:S(2)}, u32[]{:S(2)}) collective-permute-start(f32[1,2,32,512]{3,2,1,0:T(8,128)S(1)} %get-tuple-element.37), channel_id=1, source_target_pairs={{0,1},{1,0},{2,3},{3,2},{4,5},{5,4},{6,7},{7,6},{8,9},{9,8},{10,11... | collective-permute-start | bytes 393224 | tf_op jit(solution)/shard_map/ppermute | solution.py:20
  44.5 5.2 %collective-permute-start.1 = (f32[32,2048]{1,0:T(8,128)S(1)}, f32[32,2048]{1,0:T(8,128)S(1)}, u32[]{:S(2)}, u32[]{:S(2)}) collective-permute-start(f32[32,2048]{1,0:T(8,128)S(1)} %pad_maximum_fusion.4), channel_id=1, source_target_pairs={{0,24},{1,25},{2,26},{3,27},{4,28},{5,29},{6,30},{7,31},{8,16},{9,... | collective-permute-start | bytes 786440 | tf_op jit(solution)/shard_map/ppermute | solution.py:20
  45.7 18.0 %copy-start.11 = (f32[1,2,32,512]{3,2,1,0:T(8,128)}, f32[1,2,32,512]{3,2,1,0:T(8,128)S(1)}, u32[]{:S(2)}) copy-start(f32[1,2,32,512]{3,2,1,0:T(8,128)S(1)} %collective-permute-done.16) | copy-start | bytes 393220
  45.7 6.4 %collective-permute-start.22 = (f32[32,2048]{1,0:T(8,128)S(1)}, f32[32,2048]{1,0:T(8,128)S(1)}, u32[]{:S(2)}, u32[]{:S(2)}) collective-permute-start(f32[32,2048]{1,0:T(8,128)S(1)} %collective-permute-done.21), channel_id=1, source_target_pairs={{0,1},{1,0},{2,3},{3,2},{4,5},{5,4},{6,7},{7,6},{8,9},{9,8},{10,11... | collective-permute-start | bytes 786440 | tf_op jit(solution)/shard_map/ppermute | solution.py:20
  48.6 25.0 %copy-start.14 = (s32[4]{0:T(128)S(1)}, s32[4]{0:T(128)}, u32[]{:S(2)}) copy-start(s32[4]{0:T(128)} %copy-done.13) | copy-start | bytes 52
  49.7 7.4 %collective-permute-start.17 = (f32[2,2,32,512]{3,2,1,0:T(8,128)S(1)}, f32[2,2,32,512]{3,2,1,0:T(8,128)}, u32[]{:S(2)}, u32[]{:S(2)}) collective-permute-start(f32[2,2,32,512]{3,2,1,0:T(8,128)S(1)} %pad_maximum_fusion.5), channel_id=1, source_target_pairs={{0,7},{1,2},{2,1},{3,4},{4,3},{5,6},{6,5},{7,0},{8,15},{9,10},{10,... | collective-permute-start | bytes 786440 | tf_op jit(solution)/shard_map/ppermute | solution.py:20
  52.1 8.8 %collective-permute-start.23 = (f32[32,2048]{1,0:T(8,128)S(1)}, f32[32,2048]{1,0:T(8,128)S(1)}, u32[]{:S(2)}, u32[]{:S(2)}) collective-permute-start(f32[32,2048]{1,0:T(8,128)S(1)} %collective-permute-done.22), channel_id=1, source_target_pairs={{0,7},{1,2},{2,1},{3,4},{4,3},{5,6},{6,5},{7,0},{8,15},{9,10},{10,... | collective-permute-start | bytes 786440 | tf_op jit(solution)/shard_map/ppermute | solution.py:20
  57.1 20.9 %collective-permute-start.2 = (f32[64,2048]{1,0:T(8,128)}, f32[64,2048]{1,0:T(8,128)S(1)}, u32[]{:S(2)}, u32[]{:S(2)}) collective-permute-start(f32[64,2048]{1,0:T(8,128)} %pad_maximum_fusion.2), channel_id=1, source_target_pairs={{0,1},{1,0},{2,3},{3,2},{4,5},{5,4},{6,7},{7,6},{8,9},{9,8},{10,11... | collective-permute-start | bytes 1572872 | tf_op jit(solution)/shard_map/ppermute | solution.py:20
  61.0 15.3 %collective-permute-start.18 = (f32[2,2,32,512]{3,2,1,0:T(8,128)}, f32[2,2,32,512]{3,2,1,0:T(8,128)}, u32[]{:S(2)}, u32[]{:S(2)}) collective-permute-start(f32[2,2,32,512]{3,2,1,0:T(8,128)} %collective-permute-done.17), channel_id=1, source_target_pairs={{0,1},{1,0},{2,3},{3,2},{4,5},{5,4},{6,7},{7,6},{8,9},{9,8},{10,11... | collective-permute-start | bytes 786440 | tf_op jit(solution)/shard_map/ppermute | solution.py:20
  62.4 20.7 %collective-permute-start.24 = (f32[128,2048]{1,0:T(8,128)}, f32[128,2048]{1,0:T(8,128)}, u32[]{:S(2)}, u32[]{:S(2)}) collective-permute-start(f32[128,2048]{1,0:T(8,128)} %get-tuple-element.44), channel_id=1, source_target_pairs={{0,8},{1,9},{2,10},{3,11},{4,12},{5,13},{6,14},{7,15},{8,0},{9,1},... | collective-permute-start | bytes 3145736 | tf_op jit(solution)/shard_map/ppermute | solution.py:20
  63.7 10.2 %copy-start.12 = (f32[1,2,32,512]{3,2,1,0:T(8,128)S(1)}, f32[1,2,32,512]{3,2,1,0:T(8,128)}, u32[]{:S(2)}) copy-start(f32[1,2,32,512]{3,2,1,0:T(8,128)} %copy-done.11) | copy-start | bytes 393220
  65.5 22.2 %collective-permute-start.9 = (f32[512,512]{1,0:T(8,128)S(1)}, f32[512,512]{1,0:T(8,128)S(1)}, u32[]{:S(2)}, u32[]{:S(2)}) collective-permute-start(f32[512,512]{1,0:T(8,128)S(1)} %select_select_fusion), channel_id=1, source_target_pairs={{0,32},{32,0},{64,96},{96,64},{128,160},{160,128},{192,224},{224,1... | collective-permute-start | bytes 3145736 | tf_op jit(solution)/shard_map/ppermute | solution.py:57
  76.3 6.1 %collective-permute-start.19 = (f32[2,2,32,512]{3,2,1,0:T(8,128)}, f32[2,2,32,512]{3,2,1,0:T(8,128)S(1)}, u32[]{:S(2)}, u32[]{:S(2)}) collective-permute-start(f32[2,2,32,512]{3,2,1,0:T(8,128)} %collective-permute-done.18), channel_id=1, source_target_pairs={{0,7},{1,2},{2,1},{3,4},{4,3},{5,6},{6,5},{7,0},{8,15},{9,10},{10,... | collective-permute-start | bytes 786440 | tf_op jit(solution)/shard_map/ppermute | solution.py:20
  78.0 9.6 %copy-start.9 = (f32[64,2048]{1,0:T(8,128)}, f32[64,2048]{1,0:T(8,128)S(1)}, u32[]{:S(2)}) copy-start(f32[64,2048]{1,0:T(8,128)S(1)} %collective-permute-done.2) | copy-start | bytes 1572868
  79.2 28.0 %collective-permute-start.3 = (f32[128,2048]{1,0:T(8,128)}, f32[128,2048]{1,0:T(8,128)}, u32[]{:S(2)}, u32[]{:S(2)}) collective-permute-start(f32[128,2048]{1,0:T(8,128)} %pad_maximum_fusion.1), channel_id=1, source_target_pairs={{0,7},{1,2},{2,1},{3,4},{4,3},{5,6},{6,5},{7,0},{8,15},{9,10},{10,... | collective-permute-start | bytes 3145736 | tf_op jit(solution)/shard_map/ppermute | solution.py:20
  85.9 4.9 %copy-start.10 = (f32[8,2,32,512]{3,2,1,0:T(8,128)S(1)}, f32[8,2,32,512]{3,2,1,0:T(8,128)}, u32[]{:S(2)}) copy-start(f32[8,2,32,512]{3,2,1,0:T(8,128)} %constant_dynamic-update-slice_fusion.7) | copy-start | bytes 3145732
  85.9 56.2 %collective-permute-start.25 = (f32[256,2048]{1,0:T(8,128)}, f32[256,2048]{1,0:T(8,128)}, u32[]{:S(2)}, u32[]{:S(2)}) collective-permute-start(f32[256,2048]{1,0:T(8,128)} %get-tuple-element.38), channel_id=1, source_target_pairs={{0,24},{1,25},{2,26},{3,27},{4,28},{5,29},{6,30},{7,31},{8,16},{9,... | collective-permute-start | bytes 6291464 | tf_op jit(solution)/shard_map/ppermute | solution.py:20
  90.0 1.9 %copy-start.7 = (f32[2,512,512]{2,1,0:T(8,128)S(1)}, f32[2,512,512]{2,1,0:T(8,128)}, u32[]{:S(2)}) copy-start(f32[2,512,512]{2,1,0:T(8,128)} %param.11) | copy-start | bytes 6291460
  92.9 1.0 copy-start.5
  98.1 17.9 %all-to-all-start = ((f32[32,16,128]{2,1,0:T(8,128)}), f32[32,16,128]{2,1,0:T(8,128)}, u32[]{:S(2)}, u32[]{:S(2)}) async-start(f32[32,16,128]{2,1,0:T(8,128)} %bitcast.102), calls=%async_computation | async-start | bytes 524288 | tf_op jit(solution)/shard_map/all_to_all | solution.py:142
  107.1 28.0 %collective-permute-start.4 = (f32[128,2048]{1,0:T(8,128)}, f32[128,2048]{1,0:T(8,128)}, u32[]{:S(2)}, u32[]{:S(2)}) collective-permute-start(f32[128,2048]{1,0:T(8,128)} %collective-permute-done.3), channel_id=1, source_target_pairs={{0,1},{1,0},{2,3},{3,2},{4,5},{5,4},{6,7},{7,6},{8,9},{9,8},{10,11... | collective-permute-start | bytes 3145736 | tf_op jit(solution)/shard_map/ppermute | solution.py:20
  118.5 16.6 %all-to-all-start.1 = ((f32[8,5,16,128]{3,2,1,0:T(8,128)}), f32[8,5,16,128]{3,2,1,0:T(8,128)S(1)}, u32[]{:S(2)}, u32[]{:S(2)}) async-start(f32[8,5,16,128]{3,2,1,0:T(8,128)} %copy.26), calls=%async_computation.1 | async-start | bytes 655360 | tf_op jit(solution)/shard_map/all_to_all | solution.py:145
  133.2 1.4 copy-start
  135.2 14.5 %collective-permute-start.5 = (f32[128,2048]{1,0:T(8,128)}, f32[128,2048]{1,0:T(8,128)S(1)}, u32[]{:S(2)}, u32[]{:S(2)}) collective-permute-start(f32[128,2048]{1,0:T(8,128)} %collective-permute-done.4), channel_id=1, source_target_pairs={{0,7},{1,2},{2,1},{3,4},{4,3},{5,6},{6,5},{7,0},{8,15},{9,10},{10,... | collective-permute-start | bytes 3145736 | tf_op jit(solution)/shard_map/ppermute | solution.py:20
  142.1 7.5 %copy-start.2 = (f32[512,2048]{1,0:T(8,128)S(1)}, f32[512,2048]{1,0:T(8,128)}, u32[]{:S(2)}) copy-start(f32[512,2048]{1,0:T(8,128)} %constant_dynamic-update-slice_fusion.1) | copy-start | bytes 12582916
  149.0 3.2 %copy-start.1 = (f32[1024,512]{1,0:T(8,128)S(1)}, f32[1024,512]{1,0:T(8,128)}, u32[]{:S(2)}) copy-start(f32[1024,512]{1,0:T(8,128)} %copy-done) | copy-start | bytes 6291460
  149.0 3.2 %copy-start.3 = (f32[512,2048]{1,0:T(8,128)S(1)}, f32[512,2048]{1,0:T(8,128)}, u32[]{:S(2)}) copy-start(f32[512,2048]{1,0:T(8,128)} %constant_dynamic-update-slice_fusion.23) | copy-start | bytes 12582916
  152.2 3.7 %copy-start.4 = (f32[4,512,512]{2,1,0:T(8,128)S(1)}, f32[4,512,512]{2,1,0:T(8,128)}, u32[]{:S(2)}) copy-start(f32[4,512,512]{2,1,0:T(8,128)} %param.9) | copy-start | bytes 12582916
  159.6 1.2 copy-start.6
  161.2 2.0 %copy-start.8 = (f32[4,512,512]{2,1,0:T(8,128)}, f32[4,512,512]{2,1,0:T(8,128)S(1)}, u32[]{:S(2)}) copy-start(f32[4,512,512]{2,1,0:T(8,128)S(1)} %fusion.3) | copy-start | bytes 12582916

commit v2 on v0

v2 whole, which is shorter than its diff:
```python
import jax
import jax.numpy as jnp
from jax import lax
from jax.experimental import pallas as pl
from jax.experimental.pallas import tpu as pltpu
from jax.sharding import PartitionSpec as P

ROWS, Y, Z = 8, 4, 8
COLS = Y * Z


def flat(r, y, z):
    return r * COLS + (y % Y) * Z + z % Z


def permute(x, pairs):
    return lax.ppermute(x, ("row", "col"), pairs)


def tick(*values):
    return lax.optimization_barrier(values)


def along_x(x, j, cores):
    return lax.ppermute(x, "row", [(c, 2 * j + c) for c in cores])


def along_y(x, rows, to):
    return permute(x, [(flat(r, i, k), flat(r, to[i], k)) for r in rows for i in (0, 1) for k in range(Z)])


def swap_cores(x):
    return lax.ppermute(x, "row", [(r, r ^ 1) for r in range(ROWS)])


def from_z(x, distance):
    return permute(x, [
        (flat(r, i, k + (distance if r % 2 else -distance)), flat(r, i, k))
        for r in range(ROWS) for i in range(Y) for k in range(Z)
    ])


def along_ring_x(x, step):
    return lax.ppermute(x, "row", [(r, (r + 2 * step) % ROWS) for r in range(ROWS)])


def halves(x):
    high = x.astype(jnp.bfloat16)
    return high, (x - high.astype(jnp.float32)).astype(jnp.bfloat16)


def dot3(left, right_side, dims):
    dot = lambda u, v: lax.dot_general(u, v, (dims, ((), ())), preferred_element_type=jnp.float32)
    return dot(left[0], right_side[0]) + (dot(left[0], right_side[1]) + dot(left[1], right_side[0]))


def block(i):
    return pl.ds(pl.multiple_of(i * 16, 16), 16)


def panel_kernel(where_ref, index_ref, inverse_ref, own_ref, other_ref, near_ref, own_c_ref, other_c_ref, p_ref, both_ref, t_ref, first, second, ordered, factor):
    core, chip = where_ref[0], where_ref[1]
    for k, offset in enumerate((0, -1, 1, 2)):
        at = pl.ds(pl.multiple_of(lax.rem(chip + 4 + offset, 4) * 128, 128), 128)
        own, other = (own_ref[k], other_ref[k]) if k < 3 else (own_c_ref[896:], other_c_ref[896:])
        first[:, at] = jnp.where(core == 0, own, other)
        second[:, at] = jnp.where(core == 0, other, own)
    p_ref[:512, :] = dot3(halves(inverse_ref[0]), halves(first[...]), ((1,), (0,)))
    for i in range(32):
        ordered[16 * i : 16 * i + 16, :] = p_ref[block(index_ref[i]), :]
    blocks = [(near_ref, 0)] + [(own_c_ref, i) for i in range(3)] + [(other_c_ref, i) for i in range(3)]
    for k, (ref, i) in enumerate(blocks):
        for h in range(2):
            for j in range(4):
                source = 256 * i + 128 * h + 32 * j
                factor[64 * k + 32 * h : 64 * k + 32 * h + 32, 128 * j : 128 * j + 128] = ref[source : source + 32, :]
    for j in range(4):
        own, other = (ref[768 + 32 * j : 800 + 32 * j, :] for ref in (own_c_ref, other_c_ref))
        factor[448:480, 128 * j : 128 * j + 128] = jnp.where(core == 1, own, other)
        factor[480:512, 128 * j : 128 * j + 128] = jnp.where(core == 1, other, own)
    coupling = dot3(halves(factor[...]), halves(ordered[...]), ((0,), (0,)))
    p_ref[512:, :] = dot3(halves(inverse_ref[1]), halves(second[...] - coupling), ((1,), (0,)))
    both_ref[:, :512], both_ref[:, 512:] = halves(p_ref[...])
    at = pl.ds(pl.multiple_of(chip * 128, 128), 128)
    for i in range(32):
        t_ref[i] = p_ref[block(2 * i + core), at]


def call(kernel, n_scalars, outs, scratch, *args):
    whole = lambda x: pl.BlockSpec(x.shape, lambda i, *s: (0,) * len(x.shape))
    return pl.pallas_call(
        kernel,
        out_shape=outs,
        grid_spec=pltpu.PrefetchScalarGridSpec(
            num_scalar_prefetch=n_scalars,
            grid=(1,),
            in_specs=[whole(x) for x in args[n_scalars:]],
            out_specs=jax.tree.map(whole, outs),
            scratch_shapes=scratch,
        ),
        compiler_params=pltpu.CompilerParams(vmem_limit_bytes=24 * 2**20),
        cost_estimate=pl.CostEstimate(flops=6 * 512**3, bytes_accessed=4 * 2**20, transcendentals=0),
    )(*args)


def update_kernel(where_ref, a_ref, both_ref, p_ref, l_ref, o_ref):
    row, step = where_ref[2], pl.program_id(0)
    high, low = halves(l_ref[...])
    dims = (((0,), (0,)), ((), ()))
    first = lax.dot_general(high, both_ref[...], dims, preferred_element_type=jnp.float32)
    second = lax.dot_general(low, both_ref[:, :512], dims, preferred_element_type=jnp.float32)
    o_ref[...] = a_ref[...] - (first[:, :512] + (first[:, 512:] + second))

    @pl.when((step == 0) & (row < 2))
    def _():
        o_ref[...] = p_ref[...]


def update(where, a, both, panels, factor):
    depth, columns = panels.shape
    width = 512
    rows = a.shape[0]
    return pl.pallas_call(
        update_kernel,
        out_shape=jax.ShapeDtypeStruct(a.shape, a.dtype),
        grid_spec=pltpu.PrefetchScalarGridSpec(
            num_scalar_prefetch=1,
            grid=(rows // width,),
            in_specs=[
                pl.BlockSpec((width, columns), lambda i, s: (i, 0)),
                pl.BlockSpec(both.shape, lambda i, s: (0, 0)),
                pl.BlockSpec((512, columns), lambda i, s: (jnp.minimum(s[2], 1), 0)),
                pl.BlockSpec((depth, width), lambda i, s: (0, i)),
            ],
            out_specs=pl.BlockSpec((width, columns), lambda i, s: (i, 0)),
        ),
        compiler_params=pltpu.CompilerParams(vmem_limit_bytes=40 * 2**20),
        cost_estimate=pl.CostEstimate(flops=6 * depth * columns * rows, bytes_accessed=20 * 2**20, transcendentals=0),
    )(where, a, both, panels, factor)


def right_kernel(where_ref, inverse_ref, in_ref, l_ref, right_ref, own, y_ref):
    step = pl.program_id(0)

    @pl.when(step == 0)
    def _():
        for j in range(4):
            for c in range(2):
                for t in range(5):
                    own[t, 16 * c : 16 * c + 16, 128 * j : 128 * j + 128] = in_ref[2 * j + c, t]
        y_ref[...] = dot3(halves(own[4]), halves(inverse_ref[0]), ((1,), (1,)))

    y = y_ref[...]
    solved = own[step] - dot3(halves(y), halves(l_ref[...]), ((1,), (0,)))
    solved = jnp.where((step == 0) & (where_ref[2] == 0), y, solved)
    for t in range(4):

        @pl.when(step == t)
        def _():
            right_ref[:, t, :] = solved


def right_panel(where, inverses, pieces, factor):
    return pl.pallas_call(
        right_kernel,
        out_shape=jax.ShapeDtypeStruct((32, 4, 512), factor.dtype),
        grid_spec=pltpu.PrefetchScalarGridSpec(
            num_scalar_prefetch=1,
            grid=(4,),
            in_specs=[
                pl.BlockSpec((1, 512, 512), lambda i, s: (0, 0, 0)),
                pl.BlockSpec(pieces.shape, lambda i, s: (0, 0, 0, 0)),
                pl.BlockSpec((512, 512), lambda i, s: (0, i)),
            ],
            out_specs=pl.BlockSpec((32, 4, 512), lambda i, s: (0, 0, 0)),
            scratch_shapes=[pltpu.VMEM((5, 32, 512), jnp.float32), pltpu.VMEM((32, 512), jnp.float32)],
        ),
        compiler_params=pltpu.CompilerParams(vmem_limit_bytes=24 * 2**20),
        cost_estimate=pl.CostEstimate(flops=6 * 512 * 32 * 2048, bytes_accessed=6 * 2**20, transcendentals=0),
    )(where, inverses, pieces, factor)


def stack(*blocks):
    return jnp.concatenate(blocks, axis=0)


def on_device(a_block, l_panel, inverses):
    row, col = lax.axis_index("row"), lax.axis_index("col")
    core, chip, y, z = row % 2, row // 2, col // Z, col % Z

    where = jnp.stack([core, chip, row]).astype(jnp.int32)

    factor = lax.all_gather(l_panel.reshape(32, 2048), "col", axis=0, tiled=True)

    tile = a_block[0]
    rows = range(ROWS)
    by_chip = lambda *four: jnp.where(chip == 0, four[0], jnp.where(chip == 1, four[1], jnp.where(chip == 2, four[2], four[3])))
    by_y = lambda *four: jnp.where(y == 0, four[0], jnp.where(y == 1, four[1], jnp.where(y == 2, four[2], four[3])))

    piece = stack(*(l_panel[:, 0, 128 * j : 128 * j + 128] for j in range(4)))
    got = lax.ppermute(piece, "row", [(1, 0)])
    quarter = [tile[:, 128 * j : 128 * j + 128] for j in range(4)]
    piece = jnp.where(row == 0, got, piece)
    piece, *quarter = tick(piece, *quarter)

    c2, c1, c3 = (along_x(piece, j, (0, 1)) for j in (2, 1, 3))
    q2, q1, q3 = (along_x(quarter[j], j, (0, 1)) for j in (2, 1, 3))
    piece = by_chip(piece, c1, c2, c3)
    (piece,) = tick(piece)

    near, far, across = along_y(piece, rows, (1, 0)), along_y(piece, rows, (3, 2)), along_y(piece, rows, (2, 3))
    pair = stack(by_y(piece, near, across, far), by_y(near, piece, far, across))
    q = by_chip(quarter[0], q1, q2, q3)
    pair, q = tick(pair, q)

    p1, p4 = from_z(pair, 1), permute(jnp.where(core == 1, pair[:128], pair[128:]), [(flat(r, i, k), flat(r, i, k + 4)) for r in rows for i in range(Y) for k in range(Z)])
    below, above = along_ring_x(q, 1), along_ring_x(q, -1)
    p01 = stack(pair, p1)
    tiles = jnp.stack([q, below, above])
    p01, below, tiles = tick(p01, below, tiles)

    p23 = from_z(p01, 2)
    beyond, other_tiles = along_ring_x(below, 1), swap_cores(tiles)
    rest = stack(p1, p23, p4, beyond)
    rest, other_tiles = tick(rest, other_tiles)
    other_rest = swap_cores(rest)

    c_side = jnp.where(core == 1, 1, -1)
    c_list = (z + c_side * jnp.array((0, 1, 2, 3, -1, -2, -3, 4), jnp.int32)) % Z
    quarters = jnp.arange(4, dtype=jnp.int32)
    c_index = (c_list[:, None] * 2 + (quarters // 2)[None, :] * 16 + (quarters % 2)[None, :]).reshape(-1)
    panels, both, pieces = call(
        panel_kernel,
        2,
        (
            jax.ShapeDtypeStruct((1024, 512), jnp.float32),
            jax.ShapeDtypeStruct((1024, 1024), jnp.bfloat16),
            jax.ShapeDtypeStruct((32, 16, 128), jnp.float32),
        ),
        [pltpu.VMEM((512, 512), jnp.float32)] * 4,
        where, c_index, inverses, tiles, other_tiles, pair, rest, other_rest,
    )

    pieces = lax.all_to_all(pieces, "col", 0, 0, tiled=True).reshape(Y, Z, 16, 128)
    first_tile = jnp.broadcast_to(pieces[0, 0], (ROWS, 1, 16, 128))
    pieces = jnp.concatenate([pieces.transpose(1, 0, 2, 3), first_tile], axis=1)
    pieces = lax.all_to_all(pieces, "row", 0, 0, tiled=True)

    reduced = update(where, a_block.reshape(2048, 512), both, panels, factor)
    pieces, reduced = tick(pieces, reduced)
    right_out = right_panel(where, inverses, pieces, factor)
    return (reduced.reshape(4, 512, 512), right_out)


def solution(mesh):
    return jax.shard_map(
        on_device,
        mesh=mesh,
        in_specs=(P(None, "row", "col"), P("col", None, "row"), P()),
        out_specs=(P(None, "row", "col"), P("col", None, "row")),
        check_vma=False,
    )
```

time: 328 us -> 151 us (0.46)
  waiting for transfers between devices: 257 us -> 32.5 us
  starting transfers between devices: 10 us -> 46.9 us
  matrix products: 35.2 us -> 0 us
  Pallas kernels: 0 us -> 19.9 us
  blocking collectives: 0 us -> 18.2 us
  local copies, waits for them, and re-layouts: 5.99 us -> 16.3 us
    psum x3 -> x0, waiting for transfers between devices: 191 us -> none  [broadcast(): return lax.psum(block, axis)]
    ppermute x0 -> x18, starting transfers between devices: none -> 41.3 us  [the longest x6 15.9 us: permute(): return lax.ppermute(x, ('row', 'col'), pairs)]
    dot_general x6 -> x0, matrix products: 35.2 us -> none  [the longest x1 17.7 us: on_device(): jnp.einsum('kcr,kj->crj', l_columns, panels, precision=highest)]
    all_to_all x1, waiting for transfers between devices: 30.3 us -> 0.01 us  [on_device(): pieces = lax.all_to_all(pieces, 'row', 0, 0, tiled=True)]
    all_gather x1, waiting for transfers between devices: 35 us -> 14.1 us  [on_device(): lax.all_gather(l_panel.reshape(32, 2048), 'col', axis=0, tiled=True)]
    pallas_call x0 -> x3, Pallas kernels: none -> 19.9 us  [the longest x1 10.7 us: update(): pl.pallas_call(update_kernel, out_shape=jax.ShapeDtypeStruct(a.shape, a.d...]
    ppermute x0 -> x18, waiting for transfers between devices: none -> 18.4 us  [the longest x6 10.3 us: permute(): return lax.ppermute(x, ('row', 'col'), pairs)]
    all_to_all x0 -> x1, blocking collectives: none -> 18.2 us  [on_device(): lax.all_to_all(pieces, 'col', 0, 0, tiled=True).reshape(Y, Z, 16, 128)]
  transfers between devices with their start and end apart: 5 -> 20, of which waited for: 5 -> 7; matrix products, arithmetic and copies ran while one was open for 7% -> 3% of each run, Pallas kernels for 0% -> 11%
where the time goes in v2:
time: 151 us; the launch traced here: 150 us
  starting transfers between devices  46.9 us (31%)
  waiting for transfers between devices  32.5 us (22%)
  Pallas kernels  19.9 us (13%)
  blocking collectives  18.2 us (12%)
  local copies, waits for them, and re-layouts  16.3 us (11%)
  between operations  14.4 us (10%)
  other arithmetic  2.02 us (1%)
    all_to_all x1, blocking collectives, on_device(): lax.all_to_all(pieces, 'col', 0, 0, tiled=True).reshape(Y, Z, 16, 128)  18.2 us
    ppermute x6, starting transfers between devices, permute(): return lax.ppermute(x, ('row', 'col'), pairs)  15.9 us
    all_gather x1, waiting for transfers between devices, on_device(): lax.all_gather(l_panel.reshape(32, 2048), 'col', axis=0, tiled=True)  14.1 us
    unnamed x19, local copies, waits for them, and re-layouts  13.8 us
    pallas_call x1, Pallas kernels, update(): pl.pallas_call(update_kernel, out_shape=jax.ShapeDtypeStruct(a.shape, a.d...  10.7 us
    ppermute x6, starting transfers between devices, along_x(): return lax.ppermute(x, 'row', [(c, 2 * j + c) for c in cores])  10.3 us
    ppermute x6, waiting for transfers between devices, permute(): return lax.ppermute(x, ('row', 'col'), pairs)  10.3 us
    ppermute x2, starting transfers between devices, swap_cores(): return lax.ppermute(x, 'row', [(r, r ^ 1) for r in range(ROWS)])  7.7 us
  transfers between devices with their start and end apart: 20, of which 7 were waited for; matrix products, arithmetic and copies ran while one was open for 3% of the time, Pallas kernels for 11%

profile of v2, /device:TPU:1, one launch (start us, length us, event | category | flops | bytes accessed | tf_op | source)
XLA Modules:
  0.0 150.2 jit_solution(18237447683321311121)
XLA Ops:
  7.2 0.0 all-gather.2.cloned.1.call-start
  7.2 1.7 %copy.19 = f32[4,8,4,512]{3,1,2,0:T(8,128)} copy(f32[4,8,4,512]{3,2,1,0:T(4,128)} %bitcast.36) | data formatting | bytes 524288
  8.9 0.0 all-gather.2.cloned.1.call-update
  9.0 1.0 fusion.4
  10.0 5.1 %collective-permute-start = (f32[128,128]{1,0:T(8,128)S(1)}, f32[128,128]{1,0:T(8,128)S(1)}, u32[]{:S(2)}, u32[]{:S(2)}) collective-permute-start(f32[128,128]{1,0:T(8,128)S(1)} %pad_maximum_fusion.5), channel_id=1, source_target_pairs={{32,0},{33,1},{34,2},{35,3},{36,4},{37,5},{38,6},{39,7},{40,8},{41... | collective-permute-start | bytes 196616 | tf_op jit(solution)/shard_map/ppermute | solution.py:201
  15.1 1.3 slice_bitcast_fusion
  16.4 0.0 copy-start.8
  16.5 0.1 fusion.3
  16.6 1.4 collective-permute-start.1
  18.0 1.3 collective-permute-start.2
  19.3 1.3 collective-permute-start.3
  20.6 0.5 collective-permute-done.2
  21.1 1.2 collective-permute-done.3
  22.3 1.9 %collective-permute-start.4 = (f32[128,128]{1,0:T(8,128)S(1)}, f32[128,128]{1,0:T(8,128)S(1)}, u32[]{:S(2)}, u32[]{:S(2)}) collective-permute-start(f32[128,128]{1,0:T(8,128)S(1)} %select_select_fusion.3), channel_id=1, source_target_pairs={{0,8},{1,9},{2,10},{3,11},{4,12},{5,13},{6,14},{7,15},{8,0},{9,1},... | collective-permute-start | bytes 196616 | tf_op jit(solution)/shard_map/ppermute | solution.py:17
  24.2 2.3 %collective-permute-start.5 = (f32[128,128]{1,0:T(8,128)S(1)}, f32[128,128]{1,0:T(8,128)S(1)}, u32[]{:S(2)}, u32[]{:S(2)}) collective-permute-start(f32[128,128]{1,0:T(8,128)S(1)} %select_select_fusion.3), channel_id=1, source_target_pairs={{0,16},{1,17},{2,18},{3,19},{4,20},{5,21},{6,22},{7,23},{8,24},{9,... | collective-permute-start | bytes 196616 | tf_op jit(solution)/shard_map/ppermute | solution.py:17
  26.5 1.3 collective-permute-start.6
  27.8 1.3 collective-permute-start.7
  29.2 3.3 %collective-permute-start.8 = (f32[512,128]{1,0:T(8,128)S(1)}, f32[512,128]{1,0:T(8,128)S(1)}, u32[]{:S(2)}, u32[]{:S(2)}) collective-permute-start(f32[512,128]{1,0:T(8,128)S(1)} %get-tuple-element.22), channel_id=1, source_target_pairs={{0,128},{32,160},{1,129},{33,161},{2,130},{34,162},{3,131},{35,163... | collective-permute-start | bytes 786440 | tf_op jit(solution)/shard_map/ppermute | solution.py:25
  32.5 1.7 %collective-permute-start.9 = (f32[512,128]{1,0:T(8,128)S(1)}, f32[512,128]{1,0:T(8,128)S(1)}, u32[]{:S(2)}, u32[]{:S(2)}) collective-permute-start(f32[512,128]{1,0:T(8,128)S(1)} %get-tuple-element.23), channel_id=1, source_target_pairs={{0,192},{32,224},{1,193},{33,225},{2,194},{34,226},{3,195},{35,227... | collective-permute-start | bytes 786440 | tf_op jit(solution)/shard_map/ppermute | solution.py:25
  34.2 4.6 %collective-permute-done.8 = f32[512,128]{1,0:T(8,128)S(1)} collective-permute-done((f32[512,128]{1,0:T(8,128)S(1)}, f32[512,128]{1,0:T(8,128)S(1)}, u32[]{:S(2)}, u32[]{:S(2)}) %collective-permute-start.8) | collective-permute-done | bytes 262176 | tf_op jit(solution)/shard_map/ppermute | solution.py:25
  38.9 2.3 %collective-permute-start.12 = (f32[512,128]{1,0:T(8,128)S(1)}, f32[512,128]{1,0:T(8,128)S(1)}, u32[]{:S(2)}, u32[]{:S(2)}) collective-permute-start(f32[512,128]{1,0:T(8,128)S(1)} %select_select_fusion), channel_id=1, source_target_pairs={{0,192},{32,224},{64,0},{96,32},{128,64},{160,96},{192,128},{224,1... | collective-permute-start | bytes 786440 | tf_op jit(solution)/shard_map/ppermute | solution.py:44
  41.1 5.6 %collective-permute-start.10 = (f32[256,128]{1,0:T(8,128)S(1)}, f32[256,128]{1,0:T(8,128)S(1)}, u32[]{:S(2)}, u32[]{:S(2)}) collective-permute-start(f32[256,128]{1,0:T(8,128)S(1)} %pad_maximum_fusion.4.near_ref), channel_id=1, source_target_pairs={{7,0},{0,1},{1,2},{2,3},{3,4},{4,5},{5,6},{6,7},{15,8},{8,9},{9,10... | collective-permute-start | bytes 393224 | tf_op jit(solution)/shard_map/ppermute | solution.py:17
  46.7 2.1 %collective-permute-done.10 = f32[256,128]{1,0:T(8,128)S(1)} collective-permute-done((f32[256,128]{1,0:T(8,128)S(1)}, f32[256,128]{1,0:T(8,128)S(1)}, u32[]{:S(2)}, u32[]{:S(2)}) %collective-permute-start.10) | collective-permute-done | bytes 131104 | tf_op jit(solution)/shard_map/ppermute | solution.py:17
  48.9 0.1 pad_maximum_fusion.own_ref
  49.0 0.6 copy-done.7
  49.6 5.3 %collective-permute-start.16 = (f32[3,512,128]{2,1,0:T(8,128)S(1)}, f32[3,512,128]{2,1,0:T(8,128)}, u32[]{:S(2)}, u32[]{:S(2)}) collective-permute-start(f32[3,512,128]{2,1,0:T(8,128)S(1)} %pad_maximum_fusion.own_ref), channel_id=1, source_target_pairs={{0,32},{32,0},{64,96},{96,64},{128,160},{160,128},{192,224},{224,1... | collective-permute-start | bytes 2359304 | tf_op jit(solution)/shard_map/ppermute | solution.py:33
  54.9 3.9 %collective-permute-start.13 = (f32[512,128]{1,0:T(8,128)S(1)}, f32[512,128]{1,0:T(8,128)S(1)}, u32[]{:S(2)}, u32[]{:S(2)}) collective-permute-start(f32[512,128]{1,0:T(8,128)S(1)} %pad_maximum_fusion.3), channel_id=1, source_target_pairs={{6,0},{7,1},{0,2},{1,3},{2,4},{3,5},{4,6},{5,7},{14,8},{15,9},{8,1... | collective-permute-start | bytes 786440 | tf_op jit(solution)/shard_map/ppermute | solution.py:17
  58.8 1.0 collective-permute-start.14
  59.8 8.1 %collective-permute-done.14 = f32[128,128]{1,0:T(8,128)S(1)} collective-permute-done((f32[128,128]{1,0:T(8,128)S(1)}, f32[128,128]{1,0:T(8,128)S(1)}, u32[]{:S(2)}, u32[]{:S(2)}) %collective-permute-start.14) | collective-permute-done | bytes 65568 | tf_op jit(solution)/shard_map/ppermute | solution.py:17
  67.9 0.9 pad_maximum_fusion.1.own_c_ref
  68.8 2.4 %collective-permute-start.17 = (f32[1408,128]{1,0:T(8,128)}, f32[1408,128]{1,0:T(8,128)}, u32[]{:S(2)}, u32[]{:S(2)}) collective-permute-start(f32[1408,128]{1,0:T(8,128)} %pad_maximum_fusion.1.own_c_ref), channel_id=1, source_target_pairs={{0,32},{32,0},{64,96},{96,64},{128,160},{160,128},{192,224},{224,1... | collective-permute-start | bytes 2162696 | tf_op jit(solution)/shard_map/ppermute | solution.py:33
  71.2 0.1 add_add_fusion
  71.3 0.1 add.74.index_ref
  71.4 0.1 pad_add_fusion.where_ref
  71.5 1.9 %collective-permute-done.17.other_c_ref = f32[1408,128]{1,0:T(8,128)} collective-permute-done((f32[1408,128]{1,0:T(8,128)}, f32[1408,128]{1,0:T(8,128)}, u32[]{:S(2)}, u32[]{:S(2)}) %collective-permute-start.17) | collective-permute-done | bytes 720928 | tf_op jit(solution)/shard_map/ppermute | solution.py:33
  73.4 5.5 %shard_map.59 = (f32[1024,512]{1,0:T(8,128)S(1)}, bf16[1024,1024]{1,0:T(8,128)(2,1)S(1)}, f32[32,16,128]{2,1,0:T(8,128)S(1)}) custom-call(s32[3]{0:T(128)S(1)} %pad_add_fusion.where_ref, s32[32]{0:T(128)S(1)} %add.74.index_ref, f32[2,512,512]{2,1,0:T(8,128)S(1)} %copy-done.1, f32[3,512,128]{2,1,0:T(8,128)S(1)} %pad_maximum_fusion.own_ref, ...), custom_call_target="tpu_custom_call" | custom-call | flops 805306368 | bytes 4194304 | tf_op jit(solution)/shard_map/pallas_call | solution.py:91
  78.9 1.4 copy-done.3
  80.2 1.3 copy-done.5
  81.6 18.2 %all_to_all.10 = f32[32,16,128]{2,1,0:T(8,128)S(1)} all-to-all(f32[32,16,128]{2,1,0:T(8,128)S(1)} %get-tuple-element.31), channel_id=1, replica_groups=mesh['row'=8,'col'=32] {'col'}, dimensions={0} | all-to-all | bytes 524288 | tf_op jit(solution)/shard_map/all_to_all | solution.py:244
  99.8 0.8 pad_maximum_fusion.2
  100.5 5.5 %all-to-all-start.1 = ((f32[8,5,16,128]{3,2,1,0:T(8,128)}), f32[8,5,16,128]{3,2,1,0:T(8,128)S(1)}, u32[]{:S(2)}, u32[]{:S(2)}) async-start(f32[8,5,16,128]{3,2,1,0:T(8,128)} %pad_maximum_fusion.2), calls=%async_computation.1 | async-start | bytes 655360 | tf_op jit(solution)/shard_map/all_to_all | solution.py:247
  106.1 14.1 %all-gather.2.cloned.1.call-done.l_ref = f32[1024,2048]{1,0:T(8,128)} async-done(((f32[32,2048]{1,0:T(8,128)}), f32[1024,2048]{1,0:T(8,128)}) %all-gather.2.cloned.1.call-update) | async-done | bytes 8388624 | tf_op jit(solution)/shard_map/all_gather | solution.py:193
  120.1 2.2 %copy-done.2 = f32[4,512,512]{2,1,0:T(8,128)S(1)} copy-done((f32[4,512,512]{2,1,0:T(8,128)S(1)}, f32[4,512,512]{2,1,0:T(8,128)}, u32[]{:S(2)}) %copy-start.2) | copy-done | bytes 4194328
  122.3 1.6 %copy-done.4 = f32[1024,512]{1,0:T(8,128)S(1)} copy-done((f32[1024,512]{1,0:T(8,128)S(1)}, f32[1024,512]{1,0:T(8,128)}, u32[]{:S(2)}) %copy-start.4) | copy-done | bytes 2097176
  123.9 1.6 %copy-done.6 = bf16[1024,1024]{1,0:T(8,128)(2,1)S(1)} copy-done((bf16[1024,1024]{1,0:T(8,128)(2,1)S(1)}, bf16[1024,1024]{1,0:T(8,128)(2,1)}, u32[]{:S(2)}) %copy-start.6) | copy-done | bytes 2097176
  125.5 10.7 %shard_map.60 = f32[2048,512]{1,0:T(8,128)} custom-call(s32[3]{0:T(128)S(1)} %pad_add_fusion.where_ref, f32[2048,512]{1,0:T(8,128)S(1)} %bitcast.30, bf16[1024,1024]{1,0:T(8,128)(2,1)S(1)} %copy-done.6, f32[1024,512]{1,0:T(8,128)S(1)} %copy-done.4, f32[1024,2048]{1,0:T(8,128)} %all-gather.2.cloned.1.call-done.l_ref), custom_call_target="tpu_custom_call" | custom-call | flops 6442450944 | bytes 20971520 | tf_op jit(solution)/shard_map/pallas_call | solution.py:123
  136.2 3.4 %copy-done = f32[1024,2048]{1,0:T(8,128)S(1)} copy-done((f32[1024,2048]{1,0:T(8,128)S(1)}, f32[1024,2048]{1,0:T(8,128)}, u32[]{:S(2)}) %copy-start) | copy-done | bytes 8388632
  139.5 3.8 %shard_map.61 = f32[32,4,512]{2,1,0:T(4,128)} custom-call(s32[3]{0:T(128)S(1)} %pad_add_fusion.where_ref, f32[2,512,512]{2,1,0:T(8,128)S(1)} %copy-done.1, f32[8,5,16,128]{3,2,1,0:T(8,128)S(1)} %all-to-all-done.1.in_ref, f32[1024,2048]{1,0:T(8,128)S(1)} %copy-done), custom_call_target="tpu_custom_call" | custom-call | flops 201326592 | bytes 6291456 | tf_op jit(solution)/shard_map/pallas_call | solution.py:164
  (38 shorter events, 0.2 us)
Async XLA Ops:
  7.2 112.9 %all-gather.2.cloned.1.call-start = ((), (), s32[]{:S(2)}) async-start(), calls=%async_computation.2 | async-start | bytes 8650752 | tf_op jit(solution)/shard_map/all_gather | solution.py:193
  10.0 6.6 %collective-permute-start = (f32[128,128]{1,0:T(8,128)S(1)}, f32[128,128]{1,0:T(8,128)S(1)}, u32[]{:S(2)}, u32[]{:S(2)}) collective-permute-start(f32[128,128]{1,0:T(8,128)S(1)} %pad_maximum_fusion.5), channel_id=1, source_target_pairs={{32,0},{33,1},{34,2},{35,3},{36,4},{37,5},{38,6},{39,7},{40,8},{41... | collective-permute-start | bytes 196616 | tf_op jit(solution)/shard_map/ppermute | solution.py:201
  16.4 54.8 %copy-start.8 = (s32[8]{0:T(128)S(1)}, s32[8]{0:T(128)}, u32[]{:S(2)}) copy-start(s32[8]{0:T(128)} %constant.88.clone) | copy-start | bytes 100
  16.4 56.9 %copy-start.1 = (f32[2,512,512]{2,1,0:T(8,128)S(1)}, f32[2,512,512]{2,1,0:T(8,128)}, u32[]{:S(2)}) copy-start(f32[2,512,512]{2,1,0:T(8,128)} %inverse_ref.3) | copy-start | bytes 6291460
  16.6 4.1 %collective-permute-start.1 = (f32[128,128]{1,0:T(8,128)S(1)}, f32[128,128]{1,0:T(8,128)S(1)}, u32[]{:S(2)}, u32[]{:S(2)}) collective-permute-start(f32[128,128]{1,0:T(8,128)S(1)} %broadcast_select_fusion), channel_id=1, source_target_pairs={{0,64},{32,96},{1,65},{33,97},{2,66},{34,98},{3,67},{35,99},{4,68}... | collective-permute-start | bytes 196616 | tf_op jit(solution)/shard_map/ppermute | solution.py:25
  18.0 3.1 %collective-permute-start.2 = (f32[128,128]{1,0:T(8,128)S(1)}, f32[128,128]{1,0:T(8,128)S(1)}, u32[]{:S(2)}, u32[]{:S(2)}) collective-permute-start(f32[128,128]{1,0:T(8,128)S(1)} %broadcast_select_fusion), channel_id=1, source_target_pairs={{0,128},{32,160},{1,129},{33,161},{2,130},{34,162},{3,131},{35,163... | collective-permute-start | bytes 196616 | tf_op jit(solution)/shard_map/ppermute | solution.py:25
  19.3 3.0 %collective-permute-start.3 = (f32[128,128]{1,0:T(8,128)S(1)}, f32[128,128]{1,0:T(8,128)S(1)}, u32[]{:S(2)}, u32[]{:S(2)}) collective-permute-start(f32[128,128]{1,0:T(8,128)S(1)} %broadcast_select_fusion), channel_id=1, source_target_pairs={{0,192},{32,224},{1,193},{33,225},{2,194},{34,226},{3,195},{35,227... | collective-permute-start | bytes 196616 | tf_op jit(solution)/shard_map/ppermute | solution.py:25
  22.3 10.1 %collective-permute-start.4 = (f32[128,128]{1,0:T(8,128)S(1)}, f32[128,128]{1,0:T(8,128)S(1)}, u32[]{:S(2)}, u32[]{:S(2)}) collective-permute-start(f32[128,128]{1,0:T(8,128)S(1)} %select_select_fusion.3), channel_id=1, source_target_pairs={{0,8},{1,9},{2,10},{3,11},{4,12},{5,13},{6,14},{7,15},{8,0},{9,1},... | collective-permute-start | bytes 196616 | tf_op jit(solution)/shard_map/ppermute | solution.py:17
  24.2 9.9 %collective-permute-start.5 = (f32[128,128]{1,0:T(8,128)S(1)}, f32[128,128]{1,0:T(8,128)S(1)}, u32[]{:S(2)}, u32[]{:S(2)}) collective-permute-start(f32[128,128]{1,0:T(8,128)S(1)} %select_select_fusion.3), channel_id=1, source_target_pairs={{0,16},{1,17},{2,18},{3,19},{4,20},{5,21},{6,22},{7,23},{8,24},{9,... | collective-permute-start | bytes 196616 | tf_op jit(solution)/shard_map/ppermute | solution.py:17
  26.5 7.6 %collective-permute-start.6 = (f32[128,128]{1,0:T(8,128)S(1)}, f32[128,128]{1,0:T(8,128)S(1)}, u32[]{:S(2)}, u32[]{:S(2)}) collective-permute-start(f32[128,128]{1,0:T(8,128)S(1)} %select_select_fusion.3), channel_id=1, source_target_pairs={{0,24},{1,25},{2,26},{3,27},{4,28},{5,29},{6,30},{7,31},{8,16},{9,... | collective-permute-start | bytes 196616 | tf_op jit(solution)/shard_map/ppermute | solution.py:17
  27.8 6.4 %collective-permute-start.7 = (f32[512,128]{1,0:T(8,128)S(1)}, f32[512,128]{1,0:T(8,128)S(1)}, u32[]{:S(2)}, u32[]{:S(2)}) collective-permute-start(f32[512,128]{1,0:T(8,128)S(1)} %get-tuple-element.21), channel_id=1, source_target_pairs={{0,64},{32,96},{1,65},{33,97},{2,66},{34,98},{3,67},{35,99},{4,68}... | collective-permute-start | bytes 786440 | tf_op jit(solution)/shard_map/ppermute | solution.py:25
  29.2 9.7 %collective-permute-start.8 = (f32[512,128]{1,0:T(8,128)S(1)}, f32[512,128]{1,0:T(8,128)S(1)}, u32[]{:S(2)}, u32[]{:S(2)}) collective-permute-start(f32[512,128]{1,0:T(8,128)S(1)} %get-tuple-element.22), channel_id=1, source_target_pairs={{0,128},{32,160},{1,129},{33,161},{2,130},{34,162},{3,131},{35,163... | collective-permute-start | bytes 786440 | tf_op jit(solution)/shard_map/ppermute | solution.py:25
  32.5 6.4 %collective-permute-start.9 = (f32[512,128]{1,0:T(8,128)S(1)}, f32[512,128]{1,0:T(8,128)S(1)}, u32[]{:S(2)}, u32[]{:S(2)}) collective-permute-start(f32[512,128]{1,0:T(8,128)S(1)} %get-tuple-element.23), channel_id=1, source_target_pairs={{0,192},{32,224},{1,193},{33,225},{2,194},{34,226},{3,195},{35,227... | collective-permute-start | bytes 786440 | tf_op jit(solution)/shard_map/ppermute | solution.py:25
  38.9 10.0 %collective-permute-start.12 = (f32[512,128]{1,0:T(8,128)S(1)}, f32[512,128]{1,0:T(8,128)S(1)}, u32[]{:S(2)}, u32[]{:S(2)}) collective-permute-start(f32[512,128]{1,0:T(8,128)S(1)} %select_select_fusion), channel_id=1, source_target_pairs={{0,192},{32,224},{64,0},{96,32},{128,64},{160,96},{192,128},{224,1... | collective-permute-start | bytes 786440 | tf_op jit(solution)/shard_map/ppermute | solution.py:44
  41.1 7.7 %collective-permute-start.11 = (f32[512,128]{1,0:T(8,128)S(1)}, f32[512,128]{1,0:T(8,128)S(1)}, u32[]{:S(2)}, u32[]{:S(2)}) collective-permute-start(f32[512,128]{1,0:T(8,128)S(1)} %select_select_fusion), channel_id=1, source_target_pairs={{0,64},{32,96},{64,128},{96,160},{128,192},{160,224},{192,0},{224,... | collective-permute-start | bytes 786440 | tf_op jit(solution)/shard_map/ppermute | solution.py:44
  41.1 7.7 %collective-permute-start.10 = (f32[256,128]{1,0:T(8,128)S(1)}, f32[256,128]{1,0:T(8,128)S(1)}, u32[]{:S(2)}, u32[]{:S(2)}) collective-permute-start(f32[256,128]{1,0:T(8,128)S(1)} %pad_maximum_fusion.4.near_ref), channel_id=1, source_target_pairs={{7,0},{0,1},{1,2},{2,3},{3,4},{4,5},{5,6},{6,7},{15,8},{8,9},{9,10... | collective-permute-start | bytes 393224 | tf_op jit(solution)/shard_map/ppermute | solution.py:17
  48.9 0.7 copy-start.7
  49.6 19.2 %collective-permute-start.16 = (f32[3,512,128]{2,1,0:T(8,128)S(1)}, f32[3,512,128]{2,1,0:T(8,128)}, u32[]{:S(2)}, u32[]{:S(2)}) collective-permute-start(f32[3,512,128]{2,1,0:T(8,128)S(1)} %pad_maximum_fusion.own_ref), channel_id=1, source_target_pairs={{0,32},{32,0},{64,96},{96,64},{128,160},{160,128},{192,224},{224,1... | collective-permute-start | bytes 2359304 | tf_op jit(solution)/shard_map/ppermute | solution.py:33
  54.9 13.0 %collective-permute-start.13 = (f32[512,128]{1,0:T(8,128)S(1)}, f32[512,128]{1,0:T(8,128)S(1)}, u32[]{:S(2)}, u32[]{:S(2)}) collective-permute-start(f32[512,128]{1,0:T(8,128)S(1)} %pad_maximum_fusion.3), channel_id=1, source_target_pairs={{6,0},{7,1},{0,2},{1,3},{2,4},{3,5},{4,6},{5,7},{14,8},{15,9},{8,1... | collective-permute-start | bytes 786440 | tf_op jit(solution)/shard_map/ppermute | solution.py:17
  58.8 9.1 %collective-permute-start.15 = (f32[512,128]{1,0:T(8,128)}, f32[512,128]{1,0:T(8,128)S(1)}, u32[]{:S(2)}, u32[]{:S(2)}) collective-permute-start(f32[512,128]{1,0:T(8,128)} %copy-done.7), channel_id=1, source_target_pairs={{0,64},{32,96},{64,128},{96,160},{128,192},{160,224},{192,0},{224,... | collective-permute-start | bytes 786440 | tf_op jit(solution)/shard_map/ppermute | solution.py:44
  58.8 9.1 %collective-permute-start.14 = (f32[128,128]{1,0:T(8,128)S(1)}, f32[128,128]{1,0:T(8,128)S(1)}, u32[]{:S(2)}, u32[]{:S(2)}) collective-permute-start(f32[128,128]{1,0:T(8,128)S(1)} %slice_select_fusion), channel_id=1, source_target_pairs={{0,4},{1,5},{2,6},{3,7},{4,0},{5,1},{6,2},{7,3},{8,12},{9,13},{10,... | collective-permute-start | bytes 196616 | tf_op jit(solution)/shard_map/ppermute | solution.py:17
  68.8 4.6 %collective-permute-start.17 = (f32[1408,128]{1,0:T(8,128)}, f32[1408,128]{1,0:T(8,128)}, u32[]{:S(2)}, u32[]{:S(2)}) collective-permute-start(f32[1408,128]{1,0:T(8,128)} %pad_maximum_fusion.1.own_c_ref), channel_id=1, source_target_pairs={{0,32},{32,0},{64,96},{96,64},{128,160},{160,128},{192,224},{224,1... | collective-permute-start | bytes 2162696 | tf_op jit(solution)/shard_map/ppermute | solution.py:33
  78.9 1.4 copy-start.3
  80.2 1.3 copy-start.5
  100.5 35.6 %all-to-all-start.1 = ((f32[8,5,16,128]{3,2,1,0:T(8,128)}), f32[8,5,16,128]{3,2,1,0:T(8,128)S(1)}, u32[]{:S(2)}, u32[]{:S(2)}) async-start(f32[8,5,16,128]{3,2,1,0:T(8,128)} %pad_maximum_fusion.2), calls=%async_computation.1 | async-start | bytes 655360 | tf_op jit(solution)/shard_map/all_to_all | solution.py:247
  120.1 2.2 %copy-start.2 = (f32[4,512,512]{2,1,0:T(8,128)S(1)}, f32[4,512,512]{2,1,0:T(8,128)}, u32[]{:S(2)}) copy-start(f32[4,512,512]{2,1,0:T(8,128)} %param.4) | copy-start | bytes 12582916
  122.3 1.6 %copy-start.4 = (f32[1024,512]{1,0:T(8,128)S(1)}, f32[1024,512]{1,0:T(8,128)}, u32[]{:S(2)}) copy-start(f32[1024,512]{1,0:T(8,128)} %copy-done.3) | copy-start | bytes 6291460
  123.9 1.6 %copy-start.6 = (bf16[1024,1024]{1,0:T(8,128)(2,1)S(1)}, bf16[1024,1024]{1,0:T(8,128)(2,1)}, u32[]{:S(2)}) copy-start(bf16[1024,1024]{1,0:T(8,128)(2,1)} %copy-done.5) | copy-start | bytes 6291460
  136.2 3.4 %copy-start = (f32[1024,2048]{1,0:T(8,128)S(1)}, f32[1024,2048]{1,0:T(8,128)}, u32[]{:S(2)}) copy-start(f32[1024,2048]{1,0:T(8,128)} %all-gather.2.cloned.1.call-done.l_ref) | copy-start | bytes 25165828
Sparse Core Ops, SparseCore 0:
  10.6 109.4 all-gather.1

commit v3 on v2

--- a/solution.py
+++ b/solution.py
@@ -103,44 +103,8 @@
     )(*args)
 
 
-def update_kernel(where_ref, a_ref, both_ref, p_ref, l_ref, o_ref):
+def last_kernel(where_ref, inverse_ref, in_ref, a_ref, both_ref, p_ref, l_ref, o_ref, right_ref, own, y_ref):
     row, step = where_ref[2], pl.program_id(0)
-    high, low = halves(l_ref[...])
-    dims = (((0,), (0,)), ((), ()))
-    first = lax.dot_general(high, both_ref[...], dims, preferred_element_type=jnp.float32)
-    second = lax.dot_general(low, both_ref[:, :512], dims, preferred_element_type=jnp.float32)
-    o_ref[...] = a_ref[...] - (first[:, :512] + (first[:, 512:] + second))
-
-    @pl.when((step == 0) & (row < 2))
-    def _():
-        o_ref[...] = p_ref[...]
-
-
-def update(where, a, both, panels, factor):
-    depth, columns = panels.shape
-    width = 512
-    rows = a.shape[0]
-    return pl.pallas_call(
-        update_kernel,
-        out_shape=jax.ShapeDtypeStruct(a.shape, a.dtype),
-        grid_spec=pltpu.PrefetchScalarGridSpec(
-            num_scalar_prefetch=1,
-            grid=(rows // width,),
-            in_specs=[
-                pl.BlockSpec((width, columns), lambda i, s: (i, 0)),
-                pl.BlockSpec(both.shape, lambda i, s: (0, 0)),
-                pl.BlockSpec((512, columns), lambda i, s: (jnp.minimum(s[2], 1), 0)),
-                pl.BlockSpec((depth, width), lambda i, s: (0, i)),
-            ],
-            out_specs=pl.BlockSpec((width, columns), lambda i, s: (i, 0)),
-        ),
-        compiler_params=pltpu.CompilerParams(vmem_limit_bytes=40 * 2**20),
-        cost_estimate=pl.CostEstimate(flops=6 * depth * columns * rows, bytes_accessed=20 * 2**20, transcendentals=0),
-    )(where, a, both, panels, factor)
-
-
-def right_kernel(where_ref, inverse_ref, in_ref, l_ref, right_ref, own, y_ref):
-    step = pl.program_id(0)
 
     @pl.when(step == 0)
     def _():
@@ -150,9 +114,19 @@
                     own[t, 16 * c : 16 * c + 16, 128 * j : 128 * j + 128] = in_ref[2 * j + c, t]
         y_ref[...] = dot3(halves(own[4]), halves(inverse_ref[0]), ((1,), (1,)))
 
+    high, low = halves(l_ref[...])
+    dims = (((0,), (0,)), ((), ()))
+    first = lax.dot_general(high, both_ref[...], dims, preferred_element_type=jnp.float32)
+    second = lax.dot_general(low, both_ref[:, :512], dims, preferred_element_type=jnp.float32)
+    o_ref[...] = a_ref[...] - (first[:, :512] + (first[:, 512:] + second))
+
+    @pl.when((step == 0) & (row < 2))
+    def _():
+        o_ref[...] = p_ref[...]
+
     y = y_ref[...]
-    solved = own[step] - dot3(halves(y), halves(l_ref[...]), ((1,), (0,)))
-    solved = jnp.where((step == 0) & (where_ref[2] == 0), y, solved)
+    solved = own[step] - dot3(halves(y), (high[:512], low[:512]), ((1,), (0,)))
+    solved = jnp.where((step == 0) & (row == 0), y, solved)
     for t in range(4):
 
         @pl.when(step == t)
@@ -160,24 +134,33 @@
             right_ref[:, t, :] = solved
 
 
-def right_panel(where, inverses, pieces, factor):
+def last(where, inverses, pieces, a, both, panels, factor):
+    depth, columns = panels.shape
+    width = 512
+    rows = a.shape[0]
     return pl.pallas_call(
-        right_kernel,
-        out_shape=jax.ShapeDtypeStruct((32, 4, 512), factor.dtype),
+        last_kernel,
+        out_shape=(jax.ShapeDtypeStruct(a.shape, a.dtype), jax.ShapeDtypeStruct((32, 4, 512), a.dtype)),
         grid_spec=pltpu.PrefetchScalarGridSpec(
             num_scalar_prefetch=1,
-            grid=(4,),
+            grid=(rows // width,),
             in_specs=[
                 pl.BlockSpec((1, 512, 512), lambda i, s: (0, 0, 0)),
                 pl.BlockSpec(pieces.shape, lambda i, s: (0, 0, 0, 0)),
-                pl.BlockSpec((512, 512), lambda i, s: (0, i)),
+                pl.BlockSpec((width, columns), lambda i, s: (i, 0)),
+                pl.BlockSpec(both.shape, lambda i, s: (0, 0)),
+                pl.BlockSpec((512, columns), lambda i, s: (jnp.minimum(s[2], 1), 0)),
+                pl.BlockSpec((depth, width), lambda i, s: (0, i)),
             ],
-            out_specs=pl.BlockSpec((32, 4, 512), lambda i, s: (0, 0, 0)),
+            out_specs=(
+                pl.BlockSpec((width, columns), lambda i, s: (i, 0)),
+                pl.BlockSpec((32, 4, 512), lambda i, s: (0, 0, 0)),
+            ),
             scratch_shapes=[pltpu.VMEM((5, 32, 512), jnp.float32), pltpu.VMEM((32, 512), jnp.float32)],
         ),
-        compiler_params=pltpu.CompilerParams(vmem_limit_bytes=24 * 2**20),
-        cost_estimate=pl.CostEstimate(flops=6 * 512 * 32 * 2048, bytes_accessed=6 * 2**20, transcendentals=0),
-    )(where, inverses, pieces, factor)
+        compiler_params=pltpu.CompilerParams(vmem_limit_bytes=60 * 2**20),
+        cost_estimate=pl.CostEstimate(flops=6 * depth * columns * rows, bytes_accessed=20 * 2**20, transcendentals=0),
+    )(where, inverses, pieces, a, both, panels, factor)
 
 
 def stack(*blocks):
@@ -246,9 +229,7 @@
     pieces = jnp.concatenate([pieces.transpose(1, 0, 2, 3), first_tile], axis=1)
     pieces = lax.all_to_all(pieces, "row", 0, 0, tiled=True)
 
-    reduced = update(where, a_block.reshape(2048, 512), both, panels, factor)
-    pieces, reduced = tick(pieces, reduced)
-    right_out = right_panel(where, inverses, pieces, factor)
+    reduced, right_out = last(where, inverses, pieces, a_block.reshape(2048, 512), both, panels, factor)
     return (reduced.reshape(4, 512, 512), right_out)
 
 

time: 151 us -> 142 us (0.940)
  blocking collectives: 18.2 us -> 36.4 us
  waiting for transfers between devices: 32.5 us -> 19.5 us
  local copies, waits for them, and re-layouts: 16.3 us -> 8.57 us
  starting transfers between devices: 46.9 us -> 43.6 us
  other arithmetic: 2.02 us -> 0.43 us
    all_gather x1, waiting for transfers between devices: 14.1 us -> 0.01 us  [on_device(): lax.all_gather(l_panel.reshape(32, 2048), 'col', axis=0, tiled=True)]
    all_to_all x0 -> x1, blocking collectives: none -> 12.6 us  [on_device(): pieces = lax.all_to_all(pieces, 'row', 0, 0, tiled=True)]
    unnamed x19 -> x11, local copies, waits for them, and re-layouts: 13.8 us -> 6.11 us
    all_to_all x1, blocking collectives: 18.2 us -> 23.8 us  [on_device(): lax.all_to_all(pieces, 'col', 0, 0, tiled=True).reshape(Y, Z, 16, 128)]
    all_to_all x1 -> x0, starting transfers between devices: 5.51 us -> none  [on_device(): pieces = lax.all_to_all(pieces, 'row', 0, 0, tiled=True)]
    ppermute x6, starting transfers between devices: 15.9 us -> 19.1 us  [permute(): return lax.ppermute(x, ('row', 'col'), pairs)]
    ppermute x6, waiting for transfers between devices: 6.24 us -> 8.45 us  [along_x(): return lax.ppermute(x, 'row', [(c, 2 * j + c) for c in cores])]
    pallas_call x2 -> x1, Pallas kernels: 14.4 us -> 14.6 us  [last(): pl.pallas_call(last_kernel, out_shape=(jax.ShapeDtypeStruct(a.shape, a.dt...]
  transfers between devices with their start and end apart: 20 -> 19, of which waited for: 7 -> 6; matrix products, arithmetic and copies ran while one was open for 3% -> 2% of each run, Pallas kernels for 11% -> 3%
where the time goes in v3:
time: 142 us; the launch traced here: 141 us
  starting transfers between devices  43.6 us (31%)
  blocking collectives  36.4 us (26%)
  waiting for transfers between devices  19.5 us (14%)
  Pallas kernels  18.6 us (13%)
  between operations  14.4 us (10%)
  local copies, waits for them, and re-layouts  8.57 us (6%)
    all_to_all x1, blocking collectives, on_device(): lax.all_to_all(pieces, 'col', 0, 0, tiled=True).reshape(Y, Z, 16, 128)  23.8 us
    ppermute x6, starting transfers between devices, permute(): return lax.ppermute(x, ('row', 'col'), pairs)  19.1 us
    pallas_call x1, Pallas kernels, last(): pl.pallas_call(last_kernel, out_shape=(jax.ShapeDtypeStruct(a.shape, a.dt...  14.6 us
    all_to_all x1, blocking collectives, on_device(): pieces = lax.all_to_all(pieces, 'row', 0, 0, tiled=True)  12.6 us
    ppermute x6, starting transfers between devices, along_x(): return lax.ppermute(x, 'row', [(c, 2 * j + c) for c in cores])  10.7 us
    ppermute x6, waiting for transfers between devices, permute(): return lax.ppermute(x, ('row', 'col'), pairs)  9.5 us
    ppermute x6, waiting for transfers between devices, along_x(): return lax.ppermute(x, 'row', [(c, 2 * j + c) for c in cores])  8.45 us
    ppermute x2, starting transfers between devices, swap_cores(): return lax.ppermute(x, 'row', [(r, r ^ 1) for r in range(ROWS)])  6.97 us
  transfers between devices with their start and end apart: 19, of which 6 were waited for; matrix products, arithmetic and copies ran while one was open for 2% of the time, Pallas kernels for 3%

profile of v3, /device:TPU:1, one launch (start us, length us, event | category | flops | bytes accessed | tf_op | source)
XLA Modules:
  0.0 141.5 jit_solution(17349503830018018835)
XLA Ops:
  7.2 0.0 all-gather.2.cloned.1.call-start
  7.2 1.7 %copy.19 = f32[4,8,4,512]{3,1,2,0:T(8,128)} copy(f32[4,8,4,512]{3,2,1,0:T(4,128)} %bitcast.35) | data formatting | bytes 524288
  8.9 0.0 all-gather.2.cloned.1.call-update
  9.0 1.0 fusion.4
  10.0 5.1 %collective-permute-start = (f32[128,128]{1,0:T(8,128)S(1)}, f32[128,128]{1,0:T(8,128)S(1)}, u32[]{:S(2)}, u32[]{:S(2)}) collective-permute-start(f32[128,128]{1,0:T(8,128)S(1)} %pad_maximum_fusion.5), channel_id=1, source_target_pairs={{32,0},{33,1},{34,2},{35,3},{36,4},{37,5},{38,6},{39,7},{40,8},{41... | collective-permute-start | bytes 196616 | tf_op jit(solution)/shard_map/ppermute | solution.py:184
  15.1 1.3 slice_bitcast_fusion
  16.4 0.0 copy-start.4
  16.4 0.1 fusion.3
  16.6 1.3 collective-permute-start.3
  17.9 1.3 collective-permute-start.2
  19.2 1.3 collective-permute-start.1
  20.5 0.0 collective-permute-done.3
  20.5 0.0 collective-permute-done.2
  20.5 1.5 %collective-permute-done.1 = f32[128,128]{1,0:T(8,128)S(1)} collective-permute-done((f32[128,128]{1,0:T(8,128)S(1)}, f32[128,128]{1,0:T(8,128)S(1)}, u32[]{:S(2)}, u32[]{:S(2)}) %collective-permute-start.1) | collective-permute-done | bytes 65568 | tf_op jit(solution)/shard_map/ppermute | solution.py:25
  22.1 4.2 %collective-permute-start.6 = (f32[128,128]{1,0:T(8,128)S(1)}, f32[128,128]{1,0:T(8,128)S(1)}, u32[]{:S(2)}, u32[]{:S(2)}) collective-permute-start(f32[128,128]{1,0:T(8,128)S(1)} %select_select_fusion.3), channel_id=1, source_target_pairs={{0,24},{1,25},{2,26},{3,27},{4,28},{5,29},{6,30},{7,31},{8,16},{9,... | collective-permute-start | bytes 196616 | tf_op jit(solution)/shard_map/ppermute | solution.py:17
  26.3 1.5 %collective-permute-start.5 = (f32[128,128]{1,0:T(8,128)S(1)}, f32[128,128]{1,0:T(8,128)S(1)}, u32[]{:S(2)}, u32[]{:S(2)}) collective-permute-start(f32[128,128]{1,0:T(8,128)S(1)} %select_select_fusion.3), channel_id=1, source_target_pairs={{0,16},{1,17},{2,18},{3,19},{4,20},{5,21},{6,22},{7,23},{8,24},{9,... | collective-permute-start | bytes 196616 | tf_op jit(solution)/shard_map/ppermute | solution.py:17
  27.8 2.3 %collective-permute-start.4 = (f32[128,128]{1,0:T(8,128)S(1)}, f32[128,128]{1,0:T(8,128)S(1)}, u32[]{:S(2)}, u32[]{:S(2)}) collective-permute-start(f32[128,128]{1,0:T(8,128)S(1)} %select_select_fusion.3), channel_id=1, source_target_pairs={{0,8},{1,9},{2,10},{3,11},{4,12},{5,13},{6,14},{7,15},{8,0},{9,1},... | collective-permute-start | bytes 196616 | tf_op jit(solution)/shard_map/ppermute | solution.py:17
  30.1 4.2 %collective-permute-start.7 = (f32[512,128]{1,0:T(8,128)S(1)}, f32[512,128]{1,0:T(8,128)S(1)}, u32[]{:S(2)}, u32[]{:S(2)}) collective-permute-start(f32[512,128]{1,0:T(8,128)S(1)} %get-tuple-element.21), channel_id=1, source_target_pairs={{0,64},{32,96},{1,65},{33,97},{2,66},{34,98},{3,67},{35,99},{4,68}... | collective-permute-start | bytes 786440 | tf_op jit(solution)/shard_map/ppermute | solution.py:25
  34.3 1.3 collective-permute-start.8
  35.6 0.0 collective-permute-done.6
  35.6 1.3 collective-permute-start.9
  37.0 0.0 collective-permute-done.5
  37.0 0.0 collective-permute-done.4
  37.0 1.3 collective-permute-done.7
  38.3 5.6 %collective-permute-done.8 = f32[512,128]{1,0:T(8,128)S(1)} collective-permute-done((f32[512,128]{1,0:T(8,128)S(1)}, f32[512,128]{1,0:T(8,128)S(1)}, u32[]{:S(2)}, u32[]{:S(2)}) %collective-permute-start.8) | collective-permute-done | bytes 262176 | tf_op jit(solution)/shard_map/ppermute | solution.py:25
  44.0 0.6 collective-permute-start.12
  44.6 0.9 collective-permute-start.11
  45.5 5.6 %collective-permute-start.10 = (f32[256,128]{1,0:T(8,128)S(1)}, f32[256,128]{1,0:T(8,128)S(1)}, u32[]{:S(2)}, u32[]{:S(2)}) collective-permute-start(f32[256,128]{1,0:T(8,128)S(1)} %pad_maximum_fusion.4.near_ref), channel_id=1, source_target_pairs={{7,0},{0,1},{1,2},{2,3},{3,4},{4,5},{5,6},{6,7},{15,8},{8,9},{9,10... | collective-permute-start | bytes 393224 | tf_op jit(solution)/shard_map/ppermute | solution.py:17
  51.1 2.1 %collective-permute-done.10 = f32[256,128]{1,0:T(8,128)S(1)} collective-permute-done((f32[256,128]{1,0:T(8,128)S(1)}, f32[256,128]{1,0:T(8,128)S(1)}, u32[]{:S(2)}, u32[]{:S(2)}) %collective-permute-start.10) | collective-permute-done | bytes 131104 | tf_op jit(solution)/shard_map/ppermute | solution.py:17
  53.2 0.0 collective-permute-done.12
  53.2 0.1 pad_maximum_fusion.own_ref
  53.3 4.8 %collective-permute-start.16 = (f32[3,512,128]{2,1,0:T(8,128)S(1)}, f32[3,512,128]{2,1,0:T(8,128)S(1)}, u32[]{:S(2)}, u32[]{:S(2)}) collective-permute-start(f32[3,512,128]{2,1,0:T(8,128)S(1)} %pad_maximum_fusion.own_ref), channel_id=1, source_target_pairs={{0,32},{32,0},{64,96},{96,64},{128,160},{160,128},{192,224},{224,1... | collective-permute-start | bytes 2359304 | tf_op jit(solution)/shard_map/ppermute | solution.py:33
  58.1 3.5 %collective-permute-start.13 = (f32[512,128]{1,0:T(8,128)S(1)}, f32[512,128]{1,0:T(8,128)S(1)}, u32[]{:S(2)}, u32[]{:S(2)}) collective-permute-start(f32[512,128]{1,0:T(8,128)S(1)} %pad_maximum_fusion.3), channel_id=1, source_target_pairs={{6,0},{7,1},{0,2},{1,3},{2,4},{3,5},{4,6},{5,7},{14,8},{15,9},{8,1... | collective-permute-start | bytes 786440 | tf_op jit(solution)/shard_map/ppermute | solution.py:17
  61.6 0.0 collective-permute-start.15
  61.7 2.0 %collective-permute-start.14 = (f32[128,128]{1,0:T(8,128)S(1)}, f32[128,128]{1,0:T(8,128)S(1)}, u32[]{:S(2)}, u32[]{:S(2)}) collective-permute-start(f32[128,128]{1,0:T(8,128)S(1)} %slice_select_fusion), channel_id=1, source_target_pairs={{0,4},{1,5},{2,6},{3,7},{4,0},{5,1},{6,2},{7,3},{8,12},{9,13},{10,... | collective-permute-start | bytes 196616 | tf_op jit(solution)/shard_map/ppermute | solution.py:17
  63.7 7.4 %collective-permute-done.14 = f32[128,128]{1,0:T(8,128)S(1)} collective-permute-done((f32[128,128]{1,0:T(8,128)S(1)}, f32[128,128]{1,0:T(8,128)S(1)}, u32[]{:S(2)}, u32[]{:S(2)}) %collective-permute-start.14) | collective-permute-done | bytes 65568 | tf_op jit(solution)/shard_map/ppermute | solution.py:17
  71.2 2.2 %collective-permute-start.17 = (f32[1408,128]{1,0:T(8,128)S(1)}, f32[1408,128]{1,0:T(8,128)S(1)}, u32[]{:S(2)}, u32[]{:S(2)}) collective-permute-start(f32[1408,128]{1,0:T(8,128)S(1)} %pad_maximum_fusion.1.own_c_ref), channel_id=1, source_target_pairs={{0,32},{32,0},{64,96},{96,64},{128,160},{160,128},{192,224},{224,1... | collective-permute-start | bytes 2162696 | tf_op jit(solution)/shard_map/ppermute | solution.py:33
  73.4 0.1 add_add_fusion
  73.5 0.1 add.74.index_ref
  73.6 0.1 pad_add_fusion.where_ref
  73.6 1.6 %collective-permute-done.17.other_c_ref = f32[1408,128]{1,0:T(8,128)S(1)} collective-permute-done((f32[1408,128]{1,0:T(8,128)S(1)}, f32[1408,128]{1,0:T(8,128)S(1)}, u32[]{:S(2)}, u32[]{:S(2)}) %collective-permute-start.17) | collective-permute-done | bytes 720928 | tf_op jit(solution)/shard_map/ppermute | solution.py:33
  75.2 1.6 %copy-done = f32[2,512,512]{2,1,0:T(8,128)S(1)} copy-done((f32[2,512,512]{2,1,0:T(8,128)S(1)}, f32[2,512,512]{2,1,0:T(8,128)}, u32[]{:S(2)}) %copy-start) | copy-done | bytes 2097176
  76.8 4.0 %shard_map.59 = (f32[1024,512]{1,0:T(8,128)S(1)}, bf16[1024,1024]{1,0:T(8,128)(2,1)S(1)}, f32[32,16,128]{2,1,0:T(8,128)S(1)}) custom-call(s32[3]{0:T(128)S(1)} %pad_add_fusion.where_ref, s32[32]{0:T(128)S(1)} %add.74.index_ref, f32[2,512,512]{2,1,0:T(8,128)S(1)} %copy-done, f32[3,512,128]{2,1,0:T(8,128)S(1)} %pad_maximum_fusion.own_ref, ...), custom_call_target="tpu_custom_call" | custom-call | flops 805306368 | bytes 4194304 | tf_op jit(solution)/shard_map/pallas_call | solution.py:91
  80.8 1.3 copy-done.2
  82.2 1.4 copy-done.3
  83.5 23.8 %all_to_all.10 = f32[32,16,128]{2,1,0:T(8,128)S(1)} all-to-all(f32[32,16,128]{2,1,0:T(8,128)S(1)} %get-tuple-element.31), channel_id=1, replica_groups=mesh['row'=8,'col'=32] {'col'}, dimensions={0} | all-to-all | bytes 524288 | tf_op jit(solution)/shard_map/all_to_all | solution.py:227
  107.4 12.6 %all_to_all.11.in_ref = f32[8,5,16,128]{3,2,1,0:T(8,128)} all-to-all(f32[8,5,16,128]{3,2,1,0:T(8,128)S(1)} %pad_maximum_fusion.2), channel_id=1, replica_groups=mesh['row'=8,'col'=32] {'row'}, dimensions={0} | all-to-all | bytes 655360 | tf_op jit(solution)/shard_map/all_to_all | solution.py:230
  120.0 14.6 %shard_map.60 = (f32[2048,512]{1,0:T(8,128)}, f32[32,4,512]{2,1,0:T(4,128)}) custom-call(s32[3]{0:T(128)} %copy-done.1, f32[2,512,512]{2,1,0:T(8,128)} %inverse_ref.3, f32[8,5,16,128]{3,2,1,0:T(8,128)} %all_to_all.11.in_ref, f32[2048,512]{1,0:T(8,128)} %bitcast.36, bf16[1024,1024]{1,0:T(8,128)(2,1)} %copy-done.3, f32[1024,512]{1,0:T(8,128)} %copy-done.2, ...), custom_call_target="tpu_custom_call" | custom-call | flops 6442450944 | bytes 20971520 | tf_op jit(solution)/shard_map/pallas_call | solution.py:141
  (28 shorter events, 0.3 us)
Async XLA Ops:
  7.2 112.8 %all-gather.2.cloned.1.call-start = ((), (), s32[]{:S(2)}) async-start(), calls=%async_computation.2 | async-start | bytes 8650752 | tf_op jit(solution)/shard_map/all_gather | solution.py:176
  10.0 6.6 %collective-permute-start = (f32[128,128]{1,0:T(8,128)S(1)}, f32[128,128]{1,0:T(8,128)S(1)}, u32[]{:S(2)}, u32[]{:S(2)}) collective-permute-start(f32[128,128]{1,0:T(8,128)S(1)} %pad_maximum_fusion.5), channel_id=1, source_target_pairs={{32,0},{33,1},{34,2},{35,3},{36,4},{37,5},{38,6},{39,7},{40,8},{41... | collective-permute-start | bytes 196616 | tf_op jit(solution)/shard_map/ppermute | solution.py:184
  16.4 56.9 %copy-start.4 = (s32[8]{0:T(128)S(1)}, s32[8]{0:T(128)}, u32[]{:S(2)}) copy-start(s32[8]{0:T(128)} %constant.88.clone) | copy-start | bytes 100
  16.6 3.9 %collective-permute-start.3 = (f32[128,128]{1,0:T(8,128)S(1)}, f32[128,128]{1,0:T(8,128)S(1)}, u32[]{:S(2)}, u32[]{:S(2)}) collective-permute-start(f32[128,128]{1,0:T(8,128)S(1)} %broadcast_select_fusion), channel_id=1, source_target_pairs={{0,192},{32,224},{1,193},{33,225},{2,194},{34,226},{3,195},{35,227... | collective-permute-start | bytes 196616 | tf_op jit(solution)/shard_map/ppermute | solution.py:25
  17.9 2.6 %collective-permute-start.2 = (f32[128,128]{1,0:T(8,128)S(1)}, f32[128,128]{1,0:T(8,128)S(1)}, u32[]{:S(2)}, u32[]{:S(2)}) collective-permute-start(f32[128,128]{1,0:T(8,128)S(1)} %broadcast_select_fusion), channel_id=1, source_target_pairs={{0,128},{32,160},{1,129},{33,161},{2,130},{34,162},{3,131},{35,163... | collective-permute-start | bytes 196616 | tf_op jit(solution)/shard_map/ppermute | solution.py:25
  19.2 2.9 %collective-permute-start.1 = (f32[128,128]{1,0:T(8,128)S(1)}, f32[128,128]{1,0:T(8,128)S(1)}, u32[]{:S(2)}, u32[]{:S(2)}) collective-permute-start(f32[128,128]{1,0:T(8,128)S(1)} %broadcast_select_fusion), channel_id=1, source_target_pairs={{0,64},{32,96},{1,65},{33,97},{2,66},{34,98},{3,67},{35,99},{4,68}... | collective-permute-start | bytes 196616 | tf_op jit(solution)/shard_map/ppermute | solution.py:25
  22.1 13.6 %collective-permute-start.6 = (f32[128,128]{1,0:T(8,128)S(1)}, f32[128,128]{1,0:T(8,128)S(1)}, u32[]{:S(2)}, u32[]{:S(2)}) collective-permute-start(f32[128,128]{1,0:T(8,128)S(1)} %select_select_fusion.3), channel_id=1, source_target_pairs={{0,24},{1,25},{2,26},{3,27},{4,28},{5,29},{6,30},{7,31},{8,16},{9,... | collective-permute-start | bytes 196616 | tf_op jit(solution)/shard_map/ppermute | solution.py:17
  26.3 10.7 %collective-permute-start.5 = (f32[128,128]{1,0:T(8,128)S(1)}, f32[128,128]{1,0:T(8,128)S(1)}, u32[]{:S(2)}, u32[]{:S(2)}) collective-permute-start(f32[128,128]{1,0:T(8,128)S(1)} %select_select_fusion.3), channel_id=1, source_target_pairs={{0,16},{1,17},{2,18},{3,19},{4,20},{5,21},{6,22},{7,23},{8,24},{9,... | collective-permute-start | bytes 196616 | tf_op jit(solution)/shard_map/ppermute | solution.py:17
  27.8 9.2 %collective-permute-start.4 = (f32[128,128]{1,0:T(8,128)S(1)}, f32[128,128]{1,0:T(8,128)S(1)}, u32[]{:S(2)}, u32[]{:S(2)}) collective-permute-start(f32[128,128]{1,0:T(8,128)S(1)} %select_select_fusion.3), channel_id=1, source_target_pairs={{0,8},{1,9},{2,10},{3,11},{4,12},{5,13},{6,14},{7,15},{8,0},{9,1},... | collective-permute-start | bytes 196616 | tf_op jit(solution)/shard_map/ppermute | solution.py:17
  30.1 8.2 %collective-permute-start.7 = (f32[512,128]{1,0:T(8,128)S(1)}, f32[512,128]{1,0:T(8,128)S(1)}, u32[]{:S(2)}, u32[]{:S(2)}) collective-permute-start(f32[512,128]{1,0:T(8,128)S(1)} %get-tuple-element.21), channel_id=1, source_target_pairs={{0,64},{32,96},{1,65},{33,97},{2,66},{34,98},{3,67},{35,99},{4,68}... | collective-permute-start | bytes 786440 | tf_op jit(solution)/shard_map/ppermute | solution.py:25
  34.3 9.6 %collective-permute-start.8 = (f32[512,128]{1,0:T(8,128)S(1)}, f32[512,128]{1,0:T(8,128)S(1)}, u32[]{:S(2)}, u32[]{:S(2)}) collective-permute-start(f32[512,128]{1,0:T(8,128)S(1)} %get-tuple-element.22), channel_id=1, source_target_pairs={{0,128},{32,160},{1,129},{33,161},{2,130},{34,162},{3,131},{35,163... | collective-permute-start | bytes 786440 | tf_op jit(solution)/shard_map/ppermute | solution.py:25
  35.6 8.3 %collective-permute-start.9 = (f32[512,128]{1,0:T(8,128)S(1)}, f32[512,128]{1,0:T(8,128)S(1)}, u32[]{:S(2)}, u32[]{:S(2)}) collective-permute-start(f32[512,128]{1,0:T(8,128)S(1)} %get-tuple-element.23), channel_id=1, source_target_pairs={{0,192},{32,224},{1,193},{33,225},{2,194},{34,226},{3,195},{35,227... | collective-permute-start | bytes 786440 | tf_op jit(solution)/shard_map/ppermute | solution.py:25
  44.0 9.2 %collective-permute-start.12 = (f32[512,128]{1,0:T(8,128)S(1)}, f32[512,128]{1,0:T(8,128)S(1)}, u32[]{:S(2)}, u32[]{:S(2)}) collective-permute-start(f32[512,128]{1,0:T(8,128)S(1)} %select_select_fusion), channel_id=1, source_target_pairs={{0,192},{32,224},{64,0},{96,32},{128,64},{160,96},{192,128},{224,1... | collective-permute-start | bytes 786440 | tf_op jit(solution)/shard_map/ppermute | solution.py:44
  44.6 8.6 %collective-permute-start.11 = (f32[512,128]{1,0:T(8,128)S(1)}, f32[512,128]{1,0:T(8,128)S(1)}, u32[]{:S(2)}, u32[]{:S(2)}) collective-permute-start(f32[512,128]{1,0:T(8,128)S(1)} %select_select_fusion), channel_id=1, source_target_pairs={{0,64},{32,96},{64,128},{96,160},{128,192},{160,224},{192,0},{224,... | collective-permute-start | bytes 786440 | tf_op jit(solution)/shard_map/ppermute | solution.py:44
  45.5 7.7 %collective-permute-start.10 = (f32[256,128]{1,0:T(8,128)S(1)}, f32[256,128]{1,0:T(8,128)S(1)}, u32[]{:S(2)}, u32[]{:S(2)}) collective-permute-start(f32[256,128]{1,0:T(8,128)S(1)} %pad_maximum_fusion.4.near_ref), channel_id=1, source_target_pairs={{7,0},{0,1},{1,2},{2,3},{3,4},{4,5},{5,6},{6,7},{15,8},{8,9},{9,10... | collective-permute-start | bytes 393224 | tf_op jit(solution)/shard_map/ppermute | solution.py:17
  53.3 17.9 %collective-permute-start.16 = (f32[3,512,128]{2,1,0:T(8,128)S(1)}, f32[3,512,128]{2,1,0:T(8,128)S(1)}, u32[]{:S(2)}, u32[]{:S(2)}) collective-permute-start(f32[3,512,128]{2,1,0:T(8,128)S(1)} %pad_maximum_fusion.own_ref), channel_id=1, source_target_pairs={{0,32},{32,0},{64,96},{96,64},{128,160},{160,128},{192,224},{224,1... | collective-permute-start | bytes 2359304 | tf_op jit(solution)/shard_map/ppermute | solution.py:33
  58.1 13.0 %collective-permute-start.13 = (f32[512,128]{1,0:T(8,128)S(1)}, f32[512,128]{1,0:T(8,128)S(1)}, u32[]{:S(2)}, u32[]{:S(2)}) collective-permute-start(f32[512,128]{1,0:T(8,128)S(1)} %pad_maximum_fusion.3), channel_id=1, source_target_pairs={{6,0},{7,1},{0,2},{1,3},{2,4},{3,5},{4,6},{5,7},{14,8},{15,9},{8,1... | collective-permute-start | bytes 786440 | tf_op jit(solution)/shard_map/ppermute | solution.py:17
  61.6 9.5 %collective-permute-start.15 = (f32[512,128]{1,0:T(8,128)S(1)}, f32[512,128]{1,0:T(8,128)S(1)}, u32[]{:S(2)}, u32[]{:S(2)}) collective-permute-start(f32[512,128]{1,0:T(8,128)S(1)} %collective-permute-done.11), channel_id=1, source_target_pairs={{0,64},{32,96},{64,128},{96,160},{128,192},{160,224},{192,0},{224,... | collective-permute-start | bytes 786440 | tf_op jit(solution)/shard_map/ppermute | solution.py:44
  61.7 9.4 %collective-permute-start.14 = (f32[128,128]{1,0:T(8,128)S(1)}, f32[128,128]{1,0:T(8,128)S(1)}, u32[]{:S(2)}, u32[]{:S(2)}) collective-permute-start(f32[128,128]{1,0:T(8,128)S(1)} %slice_select_fusion), channel_id=1, source_target_pairs={{0,4},{1,5},{2,6},{3,7},{4,0},{5,1},{6,2},{7,3},{8,12},{9,13},{10,... | collective-permute-start | bytes 196616 | tf_op jit(solution)/shard_map/ppermute | solution.py:17
  71.2 4.0 %collective-permute-start.17 = (f32[1408,128]{1,0:T(8,128)S(1)}, f32[1408,128]{1,0:T(8,128)S(1)}, u32[]{:S(2)}, u32[]{:S(2)}) collective-permute-start(f32[1408,128]{1,0:T(8,128)S(1)} %pad_maximum_fusion.1.own_c_ref), channel_id=1, source_target_pairs={{0,32},{32,0},{64,96},{96,64},{128,160},{160,128},{192,224},{224,1... | collective-permute-start | bytes 2162696 | tf_op jit(solution)/shard_map/ppermute | solution.py:33
  73.6 46.4 %copy-start.1 = (s32[3]{0:T(128)}, s32[3]{0:T(128)S(1)}, u32[]{:S(2)}) copy-start(s32[3]{0:T(128)S(1)} %pad_add_fusion.where_ref) | copy-start | bytes 40
  75.2 1.6 %copy-start = (f32[2,512,512]{2,1,0:T(8,128)S(1)}, f32[2,512,512]{2,1,0:T(8,128)}, u32[]{:S(2)}) copy-start(f32[2,512,512]{2,1,0:T(8,128)} %inverse_ref.3) | copy-start | bytes 6291460
  80.8 1.4 copy-start.2
  82.2 1.4 copy-start.3
Sparse Core Ops, SparseCore 0:
  11.2 108.2 all-gather.1

commit v4 on v3

--- a/solution.py
+++ b/solution.py
@@ -58,7 +58,7 @@
     return pl.ds(pl.multiple_of(i * 16, 16), 16)
 
 
-def panel_kernel(where_ref, index_ref, inverse_ref, own_ref, other_ref, near_ref, own_c_ref, other_c_ref, p_ref, both_ref, t_ref, first, second, ordered, factor):
+def panel_kernel(where_ref, index_ref, inverse_ref, own_ref, other_ref, near_ref, own_c_ref, other_c_ref, both_ref, t_ref, p_ref, first, second, ordered, factor):
     core, chip = where_ref[0], where_ref[1]
     for k, offset in enumerate((0, -1, 1, 2)):
         at = pl.ds(pl.multiple_of(lax.rem(chip + 4 + offset, 4) * 128, 128), 128)
@@ -103,7 +103,7 @@
     )(*args)
 
 
-def last_kernel(where_ref, inverse_ref, in_ref, a_ref, both_ref, p_ref, l_ref, o_ref, right_ref, own, y_ref):
+def last_kernel(where_ref, inverse_ref, in_ref, a_ref, both_ref, l_ref, o_ref, right_ref, own, y_ref):
     row, step = where_ref[2], pl.program_id(0)
 
     @pl.when(step == 0)
@@ -122,7 +122,8 @@
 
     @pl.when((step == 0) & (row < 2))
     def _():
-        o_ref[...] = p_ref[...]
+        at = pl.ds(pl.multiple_of(jnp.minimum(row, 1) * 512, 512), 512)
+        o_ref[...] = both_ref[at, :512].astype(jnp.float32) + both_ref[at, 512:].astype(jnp.float32)
 
     y = y_ref[...]
     solved = own[step] - dot3(halves(y), (high[:512], low[:512]), ((1,), (0,)))
@@ -134,8 +135,8 @@
             right_ref[:, t, :] = solved
 
 
-def last(where, inverses, pieces, a, both, panels, factor):
-    depth, columns = panels.shape
+def last(where, inverses, pieces, a, both, factor):
+    depth, columns = both.shape[0], both.shape[1] // 2
     width = 512
     rows = a.shape[0]
     return pl.pallas_call(
@@ -149,7 +150,6 @@
                 pl.BlockSpec(pieces.shape, lambda i, s: (0, 0, 0, 0)),
                 pl.BlockSpec((width, columns), lambda i, s: (i, 0)),
                 pl.BlockSpec(both.shape, lambda i, s: (0, 0)),
-                pl.BlockSpec((512, columns), lambda i, s: (jnp.minimum(s[2], 1), 0)),
                 pl.BlockSpec((depth, width), lambda i, s: (0, i)),
             ],
             out_specs=(
@@ -160,7 +160,7 @@
         ),
         compiler_params=pltpu.CompilerParams(vmem_limit_bytes=60 * 2**20),
         cost_estimate=pl.CostEstimate(flops=6 * depth * columns * rows, bytes_accessed=20 * 2**20, transcendentals=0),
-    )(where, inverses, pieces, a, both, panels, factor)
+    )(where, inverses, pieces, a, both, factor)
 
 
 def stack(*blocks):
@@ -212,15 +212,14 @@
     c_list = (z + c_side * jnp.array((0, 1, 2, 3, -1, -2, -3, 4), jnp.int32)) % Z
     quarters = jnp.arange(4, dtype=jnp.int32)
     c_index = (c_list[:, None] * 2 + (quarters // 2)[None, :] * 16 + (quarters % 2)[None, :]).reshape(-1)
-    panels, both, pieces = call(
+    both, pieces = call(
         panel_kernel,
         2,
         (
-            jax.ShapeDtypeStruct((1024, 512), jnp.float32),
             jax.ShapeDtypeStruct((1024, 1024), jnp.bfloat16),
             jax.ShapeDtypeStruct((32, 16, 128), jnp.float32),
         ),
-        [pltpu.VMEM((512, 512), jnp.float32)] * 4,
+        [pltpu.VMEM((1024, 512), jnp.float32)] + [pltpu.VMEM((512, 512), jnp.float32)] * 4,
         where, c_index, inverses, tiles, other_tiles, pair, rest, other_rest,
     )
 
@@ -229,7 +228,7 @@
     pieces = jnp.concatenate([pieces.transpose(1, 0, 2, 3), first_tile], axis=1)
     pieces = lax.all_to_all(pieces, "row", 0, 0, tiled=True)
 
-    reduced, right_out = last(where, inverses, pieces, a_block.reshape(2048, 512), both, panels, factor)
+    reduced, right_out = last(where, inverses, pieces, a_block.reshape(2048, 512), both, factor)
     return (reduced.reshape(4, 512, 512), right_out)
 
 

time: 142 us -> 142 us (level)
    unnamed x11 -> x9, local copies, waits for them, and re-layouts: 6.11 us -> 4.76 us
  transfers between devices with their start and end apart: 19 -> 19, of which waited for: 6 -> 7; matrix products, arithmetic and copies ran while one was open for 2% -> 2% of each run, Pallas kernels for 3% -> 3%
where the time goes in v4:
time: 142 us; the launch traced here: 141 us
  starting transfers between devices  43.6 us (31%)
  blocking collectives  36.4 us (26%)
  waiting for transfers between devices  20.8 us (15%)
  Pallas kernels  18.4 us (13%)
  between operations  14.4 us (10%)
  local copies, waits for them, and re-layouts  7.23 us (5%)
    all_to_all x1, blocking collectives, on_device(): lax.all_to_all(pieces, 'col', 0, 0, tiled=True).reshape(Y, Z, 16, 128)  23.7 us
    ppermute x6, starting transfers between devices, permute(): return lax.ppermute(x, ('row', 'col'), pairs)  19.1 us
    pallas_call x1, Pallas kernels, last(): pl.pallas_call(last_kernel, out_shape=(jax.ShapeDtypeStruct(a.shape, a.dt...  14.4 us
    all_to_all x1, blocking collectives, on_device(): pieces = lax.all_to_all(pieces, 'row', 0, 0, tiled=True)  12.7 us
    ppermute x6, starting transfers between devices, along_x(): return lax.ppermute(x, 'row', [(c, 2 * j + c) for c in cores])  10.7 us
    ppermute x6, waiting for transfers between devices, permute(): return lax.ppermute(x, ('row', 'col'), pairs)  9.5 us
    ppermute x6, waiting for transfers between devices, along_x(): return lax.ppermute(x, 'row', [(c, 2 * j + c) for c in cores])  8.45 us
    ppermute x2, starting transfers between devices, swap_cores(): return lax.ppermute(x, 'row', [(r, r ^ 1) for r in range(ROWS)])  6.97 us
  transfers between devices with their start and end apart: 19, of which 7 were waited for; matrix products, arithmetic and copies ran while one was open for 2% of the time, Pallas kernels for 3%

profile of v4, /device:TPU:1, one launch (start us, length us, event | category | flops | bytes accessed | tf_op | source)
XLA Modules:
  0.0 141.2 jit_solution(2244457360315064970)
XLA Ops:
  7.2 0.0 all-gather.2.cloned.1.call-start
  7.2 1.7 %copy.19 = f32[4,8,4,512]{3,1,2,0:T(8,128)} copy(f32[4,8,4,512]{3,2,1,0:T(4,128)} %bitcast.35) | data formatting | bytes 524288
  8.9 0.0 all-gather.2.cloned.1.call-update
  9.0 1.0 fusion.4
  10.0 5.1 %collective-permute-start = (f32[128,128]{1,0:T(8,128)S(1)}, f32[128,128]{1,0:T(8,128)S(1)}, u32[]{:S(2)}, u32[]{:S(2)}) collective-permute-start(f32[128,128]{1,0:T(8,128)S(1)} %pad_maximum_fusion.5), channel_id=1, source_target_pairs={{32,0},{33,1},{34,2},{35,3},{36,4},{37,5},{38,6},{39,7},{40,8},{41... | collective-permute-start | bytes 196616 | tf_op jit(solution)/shard_map/ppermute | solution.py:184
  15.1 1.3 slice_bitcast_fusion
  16.4 0.0 copy-start.3
  16.4 0.1 fusion.3
  16.5 0.0 collective-permute-done
  16.6 1.3 collective-permute-start.3
  17.9 1.3 collective-permute-start.2
  19.2 1.3 collective-permute-start.1
  20.5 0.0 collective-permute-done.2
  20.5 1.5 %collective-permute-done.1 = f32[128,128]{1,0:T(8,128)S(1)} collective-permute-done((f32[128,128]{1,0:T(8,128)S(1)}, f32[128,128]{1,0:T(8,128)S(1)}, u32[]{:S(2)}, u32[]{:S(2)}) %collective-permute-start.1) | collective-permute-done | bytes 65568 | tf_op jit(solution)/shard_map/ppermute | solution.py:25
  22.1 4.2 %collective-permute-start.6 = (f32[128,128]{1,0:T(8,128)S(1)}, f32[128,128]{1,0:T(8,128)S(1)}, u32[]{:S(2)}, u32[]{:S(2)}) collective-permute-start(f32[128,128]{1,0:T(8,128)S(1)} %select_select_fusion.3), channel_id=1, source_target_pairs={{0,24},{1,25},{2,26},{3,27},{4,28},{5,29},{6,30},{7,31},{8,16},{9,... | collective-permute-start | bytes 196616 | tf_op jit(solution)/shard_map/ppermute | solution.py:17
  26.3 1.5 %collective-permute-start.5 = (f32[128,128]{1,0:T(8,128)S(1)}, f32[128,128]{1,0:T(8,128)S(1)}, u32[]{:S(2)}, u32[]{:S(2)}) collective-permute-start(f32[128,128]{1,0:T(8,128)S(1)} %select_select_fusion.3), channel_id=1, source_target_pairs={{0,16},{1,17},{2,18},{3,19},{4,20},{5,21},{6,22},{7,23},{8,24},{9,... | collective-permute-start | bytes 196616 | tf_op jit(solution)/shard_map/ppermute | solution.py:17
  27.8 2.3 %collective-permute-start.4 = (f32[128,128]{1,0:T(8,128)S(1)}, f32[128,128]{1,0:T(8,128)S(1)}, u32[]{:S(2)}, u32[]{:S(2)}) collective-permute-start(f32[128,128]{1,0:T(8,128)S(1)} %select_select_fusion.3), channel_id=1, source_target_pairs={{0,8},{1,9},{2,10},{3,11},{4,12},{5,13},{6,14},{7,15},{8,0},{9,1},... | collective-permute-start | bytes 196616 | tf_op jit(solution)/shard_map/ppermute | solution.py:17
  30.1 4.2 %collective-permute-start.7 = (f32[512,128]{1,0:T(8,128)S(1)}, f32[512,128]{1,0:T(8,128)S(1)}, u32[]{:S(2)}, u32[]{:S(2)}) collective-permute-start(f32[512,128]{1,0:T(8,128)S(1)} %get-tuple-element.20), channel_id=1, source_target_pairs={{0,64},{32,96},{1,65},{33,97},{2,66},{34,98},{3,67},{35,99},{4,68}... | collective-permute-start | bytes 786440 | tf_op jit(solution)/shard_map/ppermute | solution.py:25
  34.3 1.3 collective-permute-start.8
  35.6 0.0 collective-permute-done.6
  35.6 1.3 collective-permute-start.9
  37.0 1.3 collective-permute-done.7
  38.3 5.6 %collective-permute-done.8 = f32[512,128]{1,0:T(8,128)S(1)} collective-permute-done((f32[512,128]{1,0:T(8,128)S(1)}, f32[512,128]{1,0:T(8,128)S(1)}, u32[]{:S(2)}, u32[]{:S(2)}) %collective-permute-start.8) | collective-permute-done | bytes 262176 | tf_op jit(solution)/shard_map/ppermute | solution.py:25
  43.9 0.0 collective-permute-done.9
  44.0 0.6 collective-permute-start.12
  44.6 0.9 collective-permute-start.11
  45.5 5.6 %collective-permute-start.10 = (f32[256,128]{1,0:T(8,128)S(1)}, f32[256,128]{1,0:T(8,128)S(1)}, u32[]{:S(2)}, u32[]{:S(2)}) collective-permute-start(f32[256,128]{1,0:T(8,128)S(1)} %pad_maximum_fusion.4.near_ref), channel_id=1, source_target_pairs={{7,0},{0,1},{1,2},{2,3},{3,4},{4,5},{5,6},{6,7},{15,8},{8,9},{9,10... | collective-permute-start | bytes 393224 | tf_op jit(solution)/shard_map/ppermute | solution.py:17
  51.1 2.1 %collective-permute-done.10 = f32[256,128]{1,0:T(8,128)S(1)} collective-permute-done((f32[256,128]{1,0:T(8,128)S(1)}, f32[256,128]{1,0:T(8,128)S(1)}, u32[]{:S(2)}, u32[]{:S(2)}) %collective-permute-start.10) | collective-permute-done | bytes 131104 | tf_op jit(solution)/shard_map/ppermute | solution.py:17
  53.2 0.0 collective-permute-done.11
  53.2 0.1 pad_maximum_fusion.own_ref
  53.3 4.8 %collective-permute-start.16 = (f32[3,512,128]{2,1,0:T(8,128)S(1)}, f32[3,512,128]{2,1,0:T(8,128)S(1)}, u32[]{:S(2)}, u32[]{:S(2)}) collective-permute-start(f32[3,512,128]{2,1,0:T(8,128)S(1)} %pad_maximum_fusion.own_ref), channel_id=1, source_target_pairs={{0,32},{32,0},{64,96},{96,64},{128,160},{160,128},{192,224},{224,1... | collective-permute-start | bytes 2359304 | tf_op jit(solution)/shard_map/ppermute | solution.py:33
  58.1 3.5 %collective-permute-start.13 = (f32[512,128]{1,0:T(8,128)S(1)}, f32[512,128]{1,0:T(8,128)S(1)}, u32[]{:S(2)}, u32[]{:S(2)}) collective-permute-start(f32[512,128]{1,0:T(8,128)S(1)} %pad_maximum_fusion.3), channel_id=1, source_target_pairs={{6,0},{7,1},{0,2},{1,3},{2,4},{3,5},{4,6},{5,7},{14,8},{15,9},{8,1... | collective-permute-start | bytes 786440 | tf_op jit(solution)/shard_map/ppermute | solution.py:17
  61.6 0.0 collective-permute-start.15
  61.7 2.0 %collective-permute-start.14 = (f32[128,128]{1,0:T(8,128)S(1)}, f32[128,128]{1,0:T(8,128)S(1)}, u32[]{:S(2)}, u32[]{:S(2)}) collective-permute-start(f32[128,128]{1,0:T(8,128)S(1)} %slice_select_fusion), channel_id=1, source_target_pairs={{0,4},{1,5},{2,6},{3,7},{4,0},{5,1},{6,2},{7,3},{8,12},{9,13},{10,... | collective-permute-start | bytes 196616 | tf_op jit(solution)/shard_map/ppermute | solution.py:17
  63.7 7.4 %collective-permute-done.14 = f32[128,128]{1,0:T(8,128)S(1)} collective-permute-done((f32[128,128]{1,0:T(8,128)S(1)}, f32[128,128]{1,0:T(8,128)S(1)}, u32[]{:S(2)}, u32[]{:S(2)}) %collective-permute-start.14) | collective-permute-done | bytes 65568 | tf_op jit(solution)/shard_map/ppermute | solution.py:17
  71.1 0.0 collective-permute-done.13
  71.2 2.2 %collective-permute-start.17 = (f32[1408,128]{1,0:T(8,128)S(1)}, f32[1408,128]{1,0:T(8,128)S(1)}, u32[]{:S(2)}, u32[]{:S(2)}) collective-permute-start(f32[1408,128]{1,0:T(8,128)S(1)} %pad_maximum_fusion.1.own_c_ref), channel_id=1, source_target_pairs={{0,32},{32,0},{64,96},{96,64},{128,160},{160,128},{192,224},{224,1... | collective-permute-start | bytes 2162696 | tf_op jit(solution)/shard_map/ppermute | solution.py:33
  73.4 0.1 add_add_fusion
  73.5 0.1 add.74.index_ref
  73.6 0.1 pad_add_fusion.where_ref
  73.6 1.6 %collective-permute-done.17.other_c_ref = f32[1408,128]{1,0:T(8,128)S(1)} collective-permute-done((f32[1408,128]{1,0:T(8,128)S(1)}, f32[1408,128]{1,0:T(8,128)S(1)}, u32[]{:S(2)}, u32[]{:S(2)}) %collective-permute-start.17) | collective-permute-done | bytes 720928 | tf_op jit(solution)/shard_map/ppermute | solution.py:33
  75.2 1.6 %copy-done = f32[2,512,512]{2,1,0:T(8,128)S(1)} copy-done((f32[2,512,512]{2,1,0:T(8,128)S(1)}, f32[2,512,512]{2,1,0:T(8,128)}, u32[]{:S(2)}) %copy-start) | copy-done | bytes 2097176
  76.8 3.9 %shard_map.59 = (bf16[1024,1024]{1,0:T(8,128)(2,1)S(1)}, f32[32,16,128]{2,1,0:T(8,128)S(1)}) custom-call(s32[3]{0:T(128)S(1)} %pad_add_fusion.where_ref, s32[32]{0:T(128)S(1)} %add.74.index_ref, f32[2,512,512]{2,1,0:T(8,128)S(1)} %copy-done, f32[3,512,128]{2,1,0:T(8,128)S(1)} %pad_maximum_fusion.own_ref, ...), custom_call_target="tpu_custom_call" | custom-call | flops 805306368 | bytes 4194304 | tf_op jit(solution)/shard_map/pallas_call | solution.py:91
  80.8 1.4 copy-done.2
  82.2 23.7 %all_to_all.10 = f32[32,16,128]{2,1,0:T(8,128)S(1)} all-to-all(f32[32,16,128]{2,1,0:T(8,128)S(1)} %get-tuple-element.30), channel_id=1, replica_groups=mesh['row'=8,'col'=32] {'col'}, dimensions={0} | all-to-all | bytes 524288 | tf_op jit(solution)/shard_map/all_to_all | solution.py:226
  105.9 12.7 %all_to_all.11.in_ref = f32[8,5,16,128]{3,2,1,0:T(8,128)} all-to-all(f32[8,5,16,128]{3,2,1,0:T(8,128)S(1)} %pad_maximum_fusion.2), channel_id=1, replica_groups=mesh['row'=8,'col'=32] {'row'}, dimensions={0} | all-to-all | bytes 655360 | tf_op jit(solution)/shard_map/all_to_all | solution.py:229
  118.6 1.3 all-gather.2.cloned.1.call-done.l_ref
  119.9 14.4 %shard_map.60 = (f32[2048,512]{1,0:T(8,128)}, f32[32,4,512]{2,1,0:T(4,128)}) custom-call(s32[3]{0:T(128)} %copy-done.1, f32[2,512,512]{2,1,0:T(8,128)} %inverse_ref.3, f32[8,5,16,128]{3,2,1,0:T(8,128)} %all_to_all.11.in_ref, f32[2048,512]{1,0:T(8,128)} %bitcast.36, bf16[1024,1024]{1,0:T(8,128)(2,1)} %copy-done.2, f32[1024,2048]{1,0:T(8,128)} %all-gather.2.cloned.1.call-done.l_ref), custom_call_target="tpu_custom_call" | custom-call | flops 6442450944 | bytes 20971520 | tf_op jit(solution)/shard_map/pallas_call | solution.py:142
  (26 shorter events, 0.3 us)
Async XLA Ops:
  7.2 112.7 %all-gather.2.cloned.1.call-start = ((), (), s32[]{:S(2)}) async-start(), calls=%async_computation.2 | async-start | bytes 8650752 | tf_op jit(solution)/shard_map/all_gather | solution.py:176
  10.0 6.6 %collective-permute-start = (f32[128,128]{1,0:T(8,128)S(1)}, f32[128,128]{1,0:T(8,128)S(1)}, u32[]{:S(2)}, u32[]{:S(2)}) collective-permute-start(f32[128,128]{1,0:T(8,128)S(1)} %pad_maximum_fusion.5), channel_id=1, source_target_pairs={{32,0},{33,1},{34,2},{35,3},{36,4},{37,5},{38,6},{39,7},{40,8},{41... | collective-permute-start | bytes 196616 | tf_op jit(solution)/shard_map/ppermute | solution.py:184
  16.4 56.9 %copy-start.3 = (s32[8]{0:T(128)S(1)}, s32[8]{0:T(128)}, u32[]{:S(2)}) copy-start(s32[8]{0:T(128)} %constant.88.clone) | copy-start | bytes 100
  16.6 3.9 %collective-permute-start.3 = (f32[128,128]{1,0:T(8,128)S(1)}, f32[128,128]{1,0:T(8,128)S(1)}, u32[]{:S(2)}, u32[]{:S(2)}) collective-permute-start(f32[128,128]{1,0:T(8,128)S(1)} %broadcast_select_fusion), channel_id=1, source_target_pairs={{0,192},{32,224},{1,193},{33,225},{2,194},{34,226},{3,195},{35,227... | collective-permute-start | bytes 196616 | tf_op jit(solution)/shard_map/ppermute | solution.py:25
  17.9 2.6 %collective-permute-start.2 = (f32[128,128]{1,0:T(8,128)S(1)}, f32[128,128]{1,0:T(8,128)S(1)}, u32[]{:S(2)}, u32[]{:S(2)}) collective-permute-start(f32[128,128]{1,0:T(8,128)S(1)} %broadcast_select_fusion), channel_id=1, source_target_pairs={{0,128},{32,160},{1,129},{33,161},{2,130},{34,162},{3,131},{35,163... | collective-permute-start | bytes 196616 | tf_op jit(solution)/shard_map/ppermute | solution.py:25
  19.2 2.9 %collective-permute-start.1 = (f32[128,128]{1,0:T(8,128)S(1)}, f32[128,128]{1,0:T(8,128)S(1)}, u32[]{:S(2)}, u32[]{:S(2)}) collective-permute-start(f32[128,128]{1,0:T(8,128)S(1)} %broadcast_select_fusion), channel_id=1, source_target_pairs={{0,64},{32,96},{1,65},{33,97},{2,66},{34,98},{3,67},{35,99},{4,68}... | collective-permute-start | bytes 196616 | tf_op jit(solution)/shard_map/ppermute | solution.py:25
  22.1 13.6 %collective-permute-start.6 = (f32[128,128]{1,0:T(8,128)S(1)}, f32[128,128]{1,0:T(8,128)S(1)}, u32[]{:S(2)}, u32[]{:S(2)}) collective-permute-start(f32[128,128]{1,0:T(8,128)S(1)} %select_select_fusion.3), channel_id=1, source_target_pairs={{0,24},{1,25},{2,26},{3,27},{4,28},{5,29},{6,30},{7,31},{8,16},{9,... | collective-permute-start | bytes 196616 | tf_op jit(solution)/shard_map/ppermute | solution.py:17
  26.3 10.7 %collective-permute-start.5 = (f32[128,128]{1,0:T(8,128)S(1)}, f32[128,128]{1,0:T(8,128)S(1)}, u32[]{:S(2)}, u32[]{:S(2)}) collective-permute-start(f32[128,128]{1,0:T(8,128)S(1)} %select_select_fusion.3), channel_id=1, source_target_pairs={{0,16},{1,17},{2,18},{3,19},{4,20},{5,21},{6,22},{7,23},{8,24},{9,... | collective-permute-start | bytes 196616 | tf_op jit(solution)/shard_map/ppermute | solution.py:17
  27.8 9.2 %collective-permute-start.4 = (f32[128,128]{1,0:T(8,128)S(1)}, f32[128,128]{1,0:T(8,128)S(1)}, u32[]{:S(2)}, u32[]{:S(2)}) collective-permute-start(f32[128,128]{1,0:T(8,128)S(1)} %select_select_fusion.3), channel_id=1, source_target_pairs={{0,8},{1,9},{2,10},{3,11},{4,12},{5,13},{6,14},{7,15},{8,0},{9,1},... | collective-permute-start | bytes 196616 | tf_op jit(solution)/shard_map/ppermute | solution.py:17
  30.1 8.2 %collective-permute-start.7 = (f32[512,128]{1,0:T(8,128)S(1)}, f32[512,128]{1,0:T(8,128)S(1)}, u32[]{:S(2)}, u32[]{:S(2)}) collective-permute-start(f32[512,128]{1,0:T(8,128)S(1)} %get-tuple-element.20), channel_id=1, source_target_pairs={{0,64},{32,96},{1,65},{33,97},{2,66},{34,98},{3,67},{35,99},{4,68}... | collective-permute-start | bytes 786440 | tf_op jit(solution)/shard_map/ppermute | solution.py:25
  34.3 9.6 %collective-permute-start.8 = (f32[512,128]{1,0:T(8,128)S(1)}, f32[512,128]{1,0:T(8,128)S(1)}, u32[]{:S(2)}, u32[]{:S(2)}) collective-permute-start(f32[512,128]{1,0:T(8,128)S(1)} %get-tuple-element.21), channel_id=1, source_target_pairs={{0,128},{32,160},{1,129},{33,161},{2,130},{34,162},{3,131},{35,163... | collective-permute-start | bytes 786440 | tf_op jit(solution)/shard_map/ppermute | solution.py:25
  35.6 8.3 %collective-permute-start.9 = (f32[512,128]{1,0:T(8,128)S(1)}, f32[512,128]{1,0:T(8,128)S(1)}, u32[]{:S(2)}, u32[]{:S(2)}) collective-permute-start(f32[512,128]{1,0:T(8,128)S(1)} %get-tuple-element.22), channel_id=1, source_target_pairs={{0,192},{32,224},{1,193},{33,225},{2,194},{34,226},{3,195},{35,227... | collective-permute-start | bytes 786440 | tf_op jit(solution)/shard_map/ppermute | solution.py:25
  44.0 9.2 %collective-permute-start.12 = (f32[512,128]{1,0:T(8,128)S(1)}, f32[512,128]{1,0:T(8,128)S(1)}, u32[]{:S(2)}, u32[]{:S(2)}) collective-permute-start(f32[512,128]{1,0:T(8,128)S(1)} %select_select_fusion), channel_id=1, source_target_pairs={{0,192},{32,224},{64,0},{96,32},{128,64},{160,96},{192,128},{224,1... | collective-permute-start | bytes 786440 | tf_op jit(solution)/shard_map/ppermute | solution.py:44
  44.6 8.6 %collective-permute-start.11 = (f32[512,128]{1,0:T(8,128)S(1)}, f32[512,128]{1,0:T(8,128)S(1)}, u32[]{:S(2)}, u32[]{:S(2)}) collective-permute-start(f32[512,128]{1,0:T(8,128)S(1)} %select_select_fusion), channel_id=1, source_target_pairs={{0,64},{32,96},{64,128},{96,160},{128,192},{160,224},{192,0},{224,... | collective-permute-start | bytes 786440 | tf_op jit(solution)/shard_map/ppermute | solution.py:44
  45.5 7.7 %collective-permute-start.10 = (f32[256,128]{1,0:T(8,128)S(1)}, f32[256,128]{1,0:T(8,128)S(1)}, u32[]{:S(2)}, u32[]{:S(2)}) collective-permute-start(f32[256,128]{1,0:T(8,128)S(1)} %pad_maximum_fusion.4.near_ref), channel_id=1, source_target_pairs={{7,0},{0,1},{1,2},{2,3},{3,4},{4,5},{5,6},{6,7},{15,8},{8,9},{9,10... | collective-permute-start | bytes 393224 | tf_op jit(solution)/shard_map/ppermute | solution.py:17
  53.3 17.9 %collective-permute-start.16 = (f32[3,512,128]{2,1,0:T(8,128)S(1)}, f32[3,512,128]{2,1,0:T(8,128)S(1)}, u32[]{:S(2)}, u32[]{:S(2)}) collective-permute-start(f32[3,512,128]{2,1,0:T(8,128)S(1)} %pad_maximum_fusion.own_ref), channel_id=1, source_target_pairs={{0,32},{32,0},{64,96},{96,64},{128,160},{160,128},{192,224},{224,1... | collective-permute-start | bytes 2359304 | tf_op jit(solution)/shard_map/ppermute | solution.py:33
  58.1 13.0 %collective-permute-start.13 = (f32[512,128]{1,0:T(8,128)S(1)}, f32[512,128]{1,0:T(8,128)S(1)}, u32[]{:S(2)}, u32[]{:S(2)}) collective-permute-start(f32[512,128]{1,0:T(8,128)S(1)} %pad_maximum_fusion.3), channel_id=1, source_target_pairs={{6,0},{7,1},{0,2},{1,3},{2,4},{3,5},{4,6},{5,7},{14,8},{15,9},{8,1... | collective-permute-start | bytes 786440 | tf_op jit(solution)/shard_map/ppermute | solution.py:17
  61.6 9.5 %collective-permute-start.15 = (f32[512,128]{1,0:T(8,128)S(1)}, f32[512,128]{1,0:T(8,128)S(1)}, u32[]{:S(2)}, u32[]{:S(2)}) collective-permute-start(f32[512,128]{1,0:T(8,128)S(1)} %collective-permute-done.11), channel_id=1, source_target_pairs={{0,64},{32,96},{64,128},{96,160},{128,192},{160,224},{192,0},{224,... | collective-permute-start | bytes 786440 | tf_op jit(solution)/shard_map/ppermute | solution.py:44
  61.7 9.4 %collective-permute-start.14 = (f32[128,128]{1,0:T(8,128)S(1)}, f32[128,128]{1,0:T(8,128)S(1)}, u32[]{:S(2)}, u32[]{:S(2)}) collective-permute-start(f32[128,128]{1,0:T(8,128)S(1)} %slice_select_fusion), channel_id=1, source_target_pairs={{0,4},{1,5},{2,6},{3,7},{4,0},{5,1},{6,2},{7,3},{8,12},{9,13},{10,... | collective-permute-start | bytes 196616 | tf_op jit(solution)/shard_map/ppermute | solution.py:17
  71.2 4.0 %collective-permute-start.17 = (f32[1408,128]{1,0:T(8,128)S(1)}, f32[1408,128]{1,0:T(8,128)S(1)}, u32[]{:S(2)}, u32[]{:S(2)}) collective-permute-start(f32[1408,128]{1,0:T(8,128)S(1)} %pad_maximum_fusion.1.own_c_ref), channel_id=1, source_target_pairs={{0,32},{32,0},{64,96},{96,64},{128,160},{160,128},{192,224},{224,1... | collective-permute-start | bytes 2162696 | tf_op jit(solution)/shard_map/ppermute | solution.py:33
  73.6 46.2 %copy-start.1 = (s32[3]{0:T(128)}, s32[3]{0:T(128)S(1)}, u32[]{:S(2)}) copy-start(s32[3]{0:T(128)S(1)} %pad_add_fusion.where_ref) | copy-start | bytes 40
  75.2 1.6 %copy-start = (f32[2,512,512]{2,1,0:T(8,128)S(1)}, f32[2,512,512]{2,1,0:T(8,128)}, u32[]{:S(2)}) copy-start(f32[2,512,512]{2,1,0:T(8,128)} %inverse_ref.3) | copy-start | bytes 6291460
  80.8 1.4 copy-start.2
Sparse Core Ops, SparseCore 0:
  11.2 108.6 all-gather.1
